TPU v7x, 32 devices: a whole 2x2x4 slice. The times are simulated.
32 devices in a mesh: expert: 8 (over y, x, core), dp: 4 (over z).
Axes of the slice: x: 2, y: 2, z: 4, core: 2. Of those that a mesh axis runs over, the one named last changes fastest.
Arguments:
- hidden: bfloat16 [4, 1024, 768], P('dp', 'expert'), may hold values from -6 to 6
- cotangent: bfloat16 [4, 1024, 768], P('dp', 'expert'), may hold values from -6 to 6
- norm1_gain: float32 [768], replicated, may hold values from 0.5 to 1.5
- w_query: bfloat16 [768, 768], P('dp'), may hold values from -0.21875 to 0.21875
- w_key: bfloat16 [768, 768], P('dp'), may hold values from -0.21875 to 0.21875
- w_value: bfloat16 [768, 768], P('dp'), may hold values from -0.21875 to 0.21875
- w_output: bfloat16 [768, 768], P('dp'), may hold values from -1.25 to 1.25
- bias_table: float32 [32, 12], replicated, may hold values from -6 to 6
- norm2_gain: float32 [768], replicated, may hold values from 0.5 to 1.5
- w_router: bfloat16 [768, 8], P('dp'), may hold values from -0.15625 to 0.15625
- w_in: bfloat16 [8, 768, 3072], P('expert', 'dp'), may hold values from -0.21875 to 0.21875
- w_out: bfloat16 [8, 3072, 768], P('expert', None, 'dp'), may hold values from -0.109375 to 0.109375
- expert_ids: int32 [4, 1024, 2], P('dp', 'expert'), may hold values from 0 to 7, all different within a row; in each aligned block of 128 rows (0 to 127, 128 to 255, ..., all dimensions but the last counted through in order) at most 36 rows name the same one
- keep_mask: int32 [4, 1024, 2], P('dp', 'expert'), may hold values 0 or 1
- buckets: int32 [1024], replicated, may hold values from 0 to 31
Outputs:
- output: bfloat16 [4, 1024, 768], P('dp', 'expert')
- grad_hidden: float32 [4, 1024, 768], P('dp', 'expert')
- grad_norm1_gain: float32 [768], P('dp')
- grad_w_query: float32 [768, 768], P('dp')
- grad_w_key: float32 [768, 768], P('dp')
- grad_w_value: float32 [768, 768], P('dp')
- grad_w_output: float32 [768, 768], P('dp')
- grad_bias_table: float32 [32, 12], P('dp')
- grad_norm2_gain: float32 [768], P('dp')
- grad_w_router: float32 [768, 8], P('dp')
- grad_w_in: float32 [8, 768, 3072], P('expert', 'dp')
- grad_w_out: float32 [8, 3072, 768], P('expert', None, 'dp')
Inputs may be any that keep to these rules, and one draw needn't show every extreme that they name: `expert_ids`: each position names two different experts. Among the positions of one device (aligned blocks of 128 positions of a sequence) no expert is named more than 36 times, and in some blocks one is named exactly 36 times.
All inputs are finite; a program needn't handle non-finite values. No bound on the sum of `keep_mask` on one device may be relied on, other than what follows from the above.
Results may differ from a plain program's by a relative error of at most 0.013.
Values may be sent and summed in bfloat16 or wider, within the bound.
A program may use at most 256 MiB of HBM per device.

v0:
```python
from functools import partial

import jax
import jax.numpy as jnp
from jax import lax
from jax.sharding import PartitionSpec as P

HIGHEST = lax.Precision.HIGHEST
NEGATIVE = -1e30
EPSILON = 1e-06


def rms_norm(values, scale_gain):
    return (
        values * lax.rsqrt(jnp.mean(values * values, axis=-1, keepdims=True) + EPSILON) * scale_gain
    )


def slot_targets(expert_ids, keep_flags, experts, capacity):
    flat_ids = expert_ids.reshape(-1)
    flat_keep = keep_flags.reshape(-1)
    markers = (flat_ids[:, None] == jnp.arange(experts, dtype=jnp.int32)[None, :]).astype(
        jnp.int32
    ) * flat_keep[:, None]
    earlier = jnp.cumsum(markers, axis=0) - markers
    places = jnp.sum(earlier * markers, axis=1)
    return jnp.where(flat_keep > 0, flat_ids * capacity + places, experts * capacity)


def block_scores(queries, key_heads, query_pos, key_pos, offset_bias):
    raw_scores = (
        jnp.einsum("qhd,khd->hqk", queries, key_heads, preferred_element_type=jnp.float32) * 0.125
    )
    offset = query_pos[:, None] - key_pos[None, :]
    clipped = jnp.clip(offset, 0, offset_bias.shape[1] - 1)
    bias_values = jnp.take(offset_bias, clipped, axis=1)
    return jnp.where((offset >= 0)[None], raw_scores + bias_values, NEGATIVE)


def score_grads(
    queries,
    key_heads,
    value_heads,
    grad_heads,
    log_total,
    row_dots,
    query_pos,
    key_pos,
    offset_bias,
):
    scores = block_scores(queries, key_heads, query_pos, key_pos, offset_bias)
    weights = jnp.exp(scores - log_total[:, :, None])
    grad_weights = jnp.einsum(
        "qhd,khd->hqk", grad_heads, value_heads, preferred_element_type=jnp.float32
    )
    grad_scores = (weights * (grad_weights - row_dots[:, :, None])).astype(jnp.bfloat16)
    return (grad_scores, weights.astype(jnp.bfloat16))


def diagonal_sums(values):
    head_count, rows, cols = values.shape
    width = cols + rows - 1
    flipped = values[:, :, ::-1]
    padded = jnp.pad(flipped, ((0, 0), (0, 0), (0, rows)))
    flat = padded.reshape(head_count, rows * (cols + rows))[:, : rows * width]
    return jnp.sum(flat.reshape(head_count, rows, width), axis=1)


def attend(queries, keys_all, values_all, query_pos, offset_bias, block_size, needed):
    tok_rows, head_count = (queries.shape[0], queries.shape[1])

    def key_positions(number):
        return number * block_size + jnp.arange(block_size, dtype=jnp.int32)

    def running_totals(number, running):
        running_max, running_sum = running
        key_here = lax.dynamic_slice_in_dim(keys_all, number * block_size, block_size, 0)
        scores = block_scores(queries, key_here, query_pos, key_positions(number), offset_bias)
        new_max = jnp.maximum(running_max, jnp.max(scores, axis=-1))
        running_sum = running_sum * jnp.exp(running_max - new_max) + jnp.sum(
            jnp.exp(scores - new_max[:, :, None]), axis=-1
        )
        return (new_max, running_sum)

    start_max = jnp.full((head_count, tok_rows), NEGATIVE, jnp.float32)
    start_sum = jnp.zeros((head_count, tok_rows), jnp.float32)
    running_max, running_sum = lax.fori_loop(0, needed, running_totals, (start_max, start_sum))
    log_total = running_max + jnp.log(running_sum)

    def mixing(number, running):
        rounded, lower_part = running
        key_here = lax.dynamic_slice_in_dim(keys_all, number * block_size, block_size, 0)
        value_here = lax.dynamic_slice_in_dim(values_all, number * block_size, block_size, 0)
        scores = block_scores(queries, key_here, query_pos, key_positions(number), offset_bias)
        weights = jnp.exp(scores - log_total[:, :, None])
        upper = weights.astype(jnp.bfloat16)
        lower = (weights - upper.astype(jnp.float32)).astype(jnp.bfloat16)
        rounded = rounded + jnp.einsum(
            "hqk,khd->qhd", upper, value_here, preferred_element_type=jnp.float32
        )
        lower_part = lower_part + jnp.einsum(
            "hqk,khd->qhd", lower, value_here, preferred_element_type=jnp.float32
        )
        return (rounded, lower_part)

    empty_out = jnp.zeros(queries.shape, jnp.float32)
    rounded, lower_part = lax.fori_loop(0, needed, mixing, (empty_out, empty_out))
    return (rounded, rounded + lower_part, log_total)


def attend_back(
    queries,
    keys_all,
    values_all,
    grad_heads,
    log_total,
    row_dots,
    query_pos,
    offset_bias,
    block_size,
    needed,
):
    tok_rows, head_count = (queries.shape[0], queries.shape[1])
    seq_len = keys_all.shape[0]
    query_start = query_pos[0]
    width = block_size + tok_rows - 1

    def backward_step(number, running):
        grad_queries, grad_offsets, partial_sums = running
        key_here = lax.dynamic_slice_in_dim(keys_all, number * block_size, block_size, 0)
        value_here = lax.dynamic_slice_in_dim(values_all, number * block_size, block_size, 0)
        key_pos = number * block_size + jnp.arange(block_size, dtype=jnp.int32)
        grad_scores, weights_low = score_grads(
            queries,
            key_here,
            value_here,
            grad_heads,
            log_total,
            row_dots,
            query_pos,
            key_pos,
            offset_bias,
        )
        grad_queries = grad_queries + jnp.einsum(
            "hqk,khd->qhd", grad_scores, key_here, preferred_element_type=jnp.float32
        )
        sums_here = diagonal_sums(grad_scores.astype(jnp.float32))
        place = query_start - number * block_size + tok_rows
        current = lax.dynamic_slice_in_dim(grad_offsets, place, width, 1)
        grad_offsets = lax.dynamic_update_slice_in_dim(grad_offsets, current + sums_here, place, 1)
        grad_keys = (
            jnp.einsum("hqk,qhd->khd", grad_scores, queries, preferred_element_type=jnp.float32)
            * 0.125
        )
        grad_values = jnp.einsum(
            "hqk,qhd->khd", weights_low, grad_heads, preferred_element_type=jnp.float32
        )
        joined = jnp.concatenate(
            [grad_keys.reshape(block_size, -1), grad_values.reshape(block_size, -1)], axis=1
        )
        partial_sums = lax.dynamic_update_slice_in_dim(partial_sums, joined, number * block_size, 0)
        return (grad_queries, grad_offsets, partial_sums)

    empty_grad = jnp.zeros(queries.shape, jnp.float32)
    empty_offsets = jnp.zeros((head_count, seq_len + 2 * tok_rows + block_size), jnp.float32)
    empty_sums = jnp.zeros((seq_len, 2 * queries.shape[1] * queries.shape[2]), jnp.float32)
    grad_queries, grad_offsets, partial_sums = lax.fori_loop(
        0, needed, backward_step, (empty_grad, empty_offsets, empty_sums)
    )
    first = block_size - 1 + tok_rows
    by_offset = grad_offsets[:, first : first + seq_len]
    return (grad_queries, by_offset, partial_sums)


def on_device(
    hidden,
    cotangent,
    norm1_gain,
    w_query,
    w_key,
    w_value,
    w_output,
    bias_table,
    norm2_gain,
    w_router,
    w_in,
    w_out,
    expert_ids,
    keep_mask,
    buckets,
):
    tok_rows = hidden.shape[1]
    model_width = hidden.shape[2]
    head_count = bias_table.shape[1]
    head_size = model_width // head_count
    experts = w_router.shape[1]
    capacity = 9 * tok_rows // (4 * experts)
    seq_len = buckets.shape[0]
    block_size = min(512, seq_len)
    my_index = lax.axis_index("expert")
    query_pos = my_index * tok_rows + jnp.arange(tok_rows, dtype=jnp.int32)
    needed = (my_index * tok_rows + tok_rows - 1) // block_size + 1
    bucket_onehot = (
        buckets[:, None] == jnp.arange(bias_table.shape[0], dtype=jnp.int32)[None, :]
    ).astype(jnp.float32)
    offset_bias = jnp.dot(bucket_onehot, bias_table, precision=HIGHEST).T
    query_all, key_all_w, value_all_w, output_all, router_all, first_all, second_all = (
        lax.all_gather(w_query, "dp", axis=0, tiled=True),
        lax.all_gather(w_key, "dp", axis=0, tiled=True),
        lax.all_gather(w_value, "dp", axis=0, tiled=True),
        lax.all_gather(w_output, "dp", axis=0, tiled=True),
        lax.all_gather(w_router, "dp", axis=0, tiled=True),
        lax.all_gather(w_in, "dp", axis=1, tiled=True),
        lax.all_gather(w_out, "dp", axis=2, tiled=True),
    )
    first_weight = first_all[0]
    second_weight = second_all[0]
    router = router_all.astype(jnp.float32)
    inputs = hidden[0].astype(jnp.float32)
    normed1_f, norm1_back = jax.vjp(rms_norm, inputs, norm1_gain)
    normed1 = normed1_f.astype(jnp.bfloat16)
    queries = jnp.dot(normed1, query_all, preferred_element_type=jnp.float32).astype(jnp.bfloat16)
    key_proj = jnp.dot(normed1, key_all_w, preferred_element_type=jnp.float32).astype(jnp.bfloat16)
    value_proj = jnp.dot(normed1, value_all_w, preferred_element_type=jnp.float32).astype(
        jnp.bfloat16
    )
    keys_all, values_all = (
        lax.all_gather(key_proj, "expert", axis=0, tiled=True),
        lax.all_gather(value_proj, "expert", axis=0, tiled=True),
    )
    query_heads = queries.reshape(tok_rows, head_count, head_size)
    key_heads = keys_all.reshape(seq_len, head_count, head_size)
    value_heads = values_all.reshape(seq_len, head_count, head_size)
    mixed, exact_out, log_total = attend(
        query_heads, key_heads, value_heads, query_pos, offset_bias, block_size, needed
    )
    attended = mixed.reshape(tok_rows, model_width).astype(jnp.bfloat16)
    resid = inputs + jnp.dot(attended, output_all, preferred_element_type=jnp.float32)
    chosen = (
        expert_ids[0][:, :, None] == jnp.arange(experts, dtype=jnp.int32)[None, None, :]
    ).astype(jnp.float32)
    kept = keep_mask[0].astype(jnp.float32)

    def route(resid_rows, gain_two, router_weight):
        normed = rms_norm(resid_rows, gain_two)
        probs = jax.nn.softmax(jnp.dot(normed, router_weight, precision=HIGHEST), axis=-1)
        picked = jnp.sum(probs[:, None, :] * chosen, axis=-1)
        return (normed, picked / jnp.sum(picked, axis=-1, keepdims=True) * kept)

    (normed2_f, gates), route_back = jax.vjp(route, resid, norm2_gain, router)
    normed2 = normed2_f.astype(jnp.bfloat16)
    targets = slot_targets(expert_ids[0], keep_mask[0], experts, capacity)
    spread = jnp.repeat(normed2, 2, axis=0)
    outgoing = (
        jnp.zeros((experts * capacity, model_width), jnp.bfloat16)
        .at[targets]
        .set(spread, mode="drop")
        .reshape(experts, capacity, model_width)
    )
    arrived = lax.all_to_all(outgoing, "expert", split_axis=0, concat_axis=0, tiled=True)
    pre_act = jnp.einsum("scd,df->scf", arrived, first_weight, preferred_element_type=jnp.float32)
    activated = jax.nn.gelu(pre_act, approximate=False).astype(jnp.bfloat16)
    expert_out = jnp.einsum(
        "scf,fd->scd", activated, second_weight, preferred_element_type=jnp.float32
    ).astype(jnp.bfloat16)
    expert_out, arrived, pre_act, activated = (expert_out, arrived, pre_act, activated)
    returned = lax.all_to_all(
        expert_out, "expert", split_axis=0, concat_axis=0, tiled=True
    ).reshape(experts * capacity, model_width)
    picked_rows = (
        jnp.take(returned, targets, axis=0, mode="fill", fill_value=0)
        .astype(jnp.float32)
        .reshape(tok_rows, 2, model_width)
    )
    output = (resid + jnp.sum(gates[:, :, None] * picked_rows, axis=1)).astype(jnp.bfloat16)
    grad_top = cotangent[0].astype(jnp.float32)
    grad_gates = jnp.sum(picked_rows * grad_top[:, None, :], axis=-1)
    grad_made = (
        (gates[:, :, None] * grad_top[:, None, :])
        .astype(jnp.bfloat16)
        .reshape(2 * tok_rows, model_width)
    )
    grad_outgoing = (
        jnp.zeros((experts * capacity, model_width), jnp.bfloat16)
        .at[targets]
        .set(grad_made, mode="drop")
        .reshape(experts, capacity, model_width)
    )
    grad_arrived_out = lax.all_to_all(
        grad_outgoing, "expert", split_axis=0, concat_axis=0, tiled=True
    )
    grad_act = jnp.einsum(
        "scd,fd->scf", grad_arrived_out, second_weight, preferred_element_type=jnp.float32
    )
    gelu_exact = partial(jax.nn.gelu, approximate=False)
    _, gelu_back = jax.vjp(gelu_exact, pre_act)
    grad_pre = gelu_back(grad_act)[0].astype(jnp.bfloat16)
    grad_first = jnp.einsum("scd,scf->df", arrived, grad_pre, preferred_element_type=jnp.float32)
    grad_second = jnp.einsum(
        "scf,scd->fd", activated, grad_arrived_out, preferred_element_type=jnp.float32
    )
    grad_rows = jnp.einsum(
        "scf,df->scd", grad_pre, first_weight, preferred_element_type=jnp.float32
    ).astype(jnp.bfloat16)
    expert_sums = (
        lax.psum_scatter(
            grad_first[None].astype(jnp.bfloat16), "dp", scatter_dimension=1, tiled=True
        ).astype(jnp.float32),
        lax.psum_scatter(
            grad_second[None].astype(jnp.bfloat16), "dp", scatter_dimension=2, tiled=True
        ).astype(jnp.float32),
    )
    grad_returned = lax.all_to_all(
        grad_rows, "expert", split_axis=0, concat_axis=0, tiled=True
    ).reshape(experts * capacity, model_width)
    grad_normed2 = jnp.sum(
        jnp.take(grad_returned, targets, axis=0, mode="fill", fill_value=0)
        .astype(jnp.float32)
        .reshape(tok_rows, 2, model_width),
        axis=1,
    )
    grad_resid_norm, grad_gain_two, grad_router = route_back((grad_normed2, grad_gates))
    grad_resid = grad_top + grad_resid_norm
    grad_branch = grad_resid.astype(jnp.bfloat16)
    grad_output = jnp.einsum("td,te->de", attended, grad_branch, preferred_element_type=jnp.float32)
    grad_attended = jnp.einsum(
        "te,de->td", grad_branch, output_all, preferred_element_type=jnp.float32
    ).astype(jnp.bfloat16)
    grad_heads = grad_attended.reshape(tok_rows, head_count, head_size)
    row_dots = jnp.sum(grad_heads.astype(jnp.float32) * exact_out, axis=2).T
    grad_queries, by_offset, partial_sums = attend_back(
        query_heads,
        key_heads,
        value_heads,
        grad_heads,
        log_total,
        row_dots,
        query_pos,
        offset_bias,
        block_size,
        needed,
    )
    summed = lax.psum_scatter(partial_sums, "expert", scatter_dimension=0, tiled=True)
    grad_keys = summed[:, :model_width].astype(jnp.bfloat16)
    grad_values = summed[:, model_width:].astype(jnp.bfloat16)
    grad_table = jnp.dot(bucket_onehot.T, by_offset.T, precision=HIGHEST)
    grad_query_low = (grad_queries * 0.125).reshape(tok_rows, model_width).astype(jnp.bfloat16)
    grad_query_w = jnp.einsum(
        "td,te->de", normed1, grad_query_low, preferred_element_type=jnp.float32
    )
    grad_key_w = jnp.einsum("td,te->de", normed1, grad_keys, preferred_element_type=jnp.float32)
    grad_value_w = jnp.einsum("td,te->de", normed1, grad_values, preferred_element_type=jnp.float32)
    grad_normed1 = jnp.einsum(
        "te,de->td", grad_query_low, query_all, preferred_element_type=jnp.float32
    )
    grad_normed1 = grad_normed1 + jnp.einsum(
        "te,de->td", grad_keys, key_all_w, preferred_element_type=jnp.float32
    )
    grad_normed1 = grad_normed1 + jnp.einsum(
        "te,de->td", grad_values, value_all_w, preferred_element_type=jnp.float32
    )
    grad_inputs, grad_gain_one = norm1_back(grad_normed1)
    grad_hidden = (grad_resid + grad_inputs)[None]
    mixer_sums = (
        lax.psum_scatter(grad_query_w, "dp", scatter_dimension=0, tiled=True),
        lax.psum_scatter(grad_key_w, "dp", scatter_dimension=0, tiled=True),
        lax.psum_scatter(grad_value_w, "dp", scatter_dimension=0, tiled=True),
        lax.psum_scatter(grad_output, "dp", scatter_dimension=0, tiled=True),
        lax.psum_scatter(grad_router, "dp", scatter_dimension=0, tiled=True),
        lax.psum_scatter(grad_gain_one, "dp", scatter_dimension=0, tiled=True),
        lax.psum_scatter(grad_gain_two, "dp", scatter_dimension=0, tiled=True),
        lax.psum_scatter(grad_table, "dp", scatter_dimension=0, tiled=True),
    )
    totals = lax.psum(
        (
            mixer_sums[0],
            mixer_sums[1],
            mixer_sums[2],
            mixer_sums[3],
            mixer_sums[4],
            mixer_sums[5],
            mixer_sums[6],
            mixer_sums[7],
        ),
        "expert",
    )
    return (
        output[None],
        grad_hidden,
        totals[5],
        totals[0],
        totals[1],
        totals[2],
        totals[3],
        totals[7],
        totals[6],
        totals[4],
        expert_sums[0],
        expert_sums[1],
    )


def solution(mesh):
    return jax.shard_map(
        on_device,
        mesh=mesh,
        in_specs=(
            P("dp", "expert", None),
            P("dp", "expert", None),
            P(),
            P("dp", None),
            P("dp", None),
            P("dp", None),
            P("dp", None),
            P(),
            P(),
            P("dp", None),
            P("expert", "dp", None),
            P("expert", None, "dp"),
            P("dp", "expert", None),
            P("dp", "expert", None),
            P(),
        ),
        out_specs=(
            P("dp", "expert", None),
            P("dp", "expert", None),
            P("dp"),
            P("dp", None),
            P("dp", None),
            P("dp", None),
            P("dp", None),
            P("dp", None),
            P("dp"),
            P("dp", None),
            P("expert", "dp", None),
            P("expert", None, "dp"),
        ),
        check_vma=False,
    )
```

profile of v0, /device:TPU:0, one launch (start us, length us, event | category | flops | bytes accessed | tf_op | source)
XLA Modules:
  0.0 2347.2 jit_solution(5463700734546529236)
XLA Ops:
  11.2 31.6 %all-gather.14.cloned.1.call-done = bf16[768,768]{1,0:T(8,128)(2,1)} async-done(((bf16[192,768]{1,0:T(8,128)(2,1)}), bf16[768,768]{1,0:T(8,128)(2,1)}) %all-gather.14.cloned.1.call-update) | async-done | bytes 1179664 | tf_op jit(solution)/shard_map/all_gather | solution.py:209
  45.3 28.6 %all-gather.10.cloned.1.call-done = bf16[768,768]{1,0:T(8,128)(2,1)} async-done(((bf16[192,768]{1,0:T(8,128)(2,1)}), bf16[768,768]{1,0:T(8,128)(2,1)}) %all-gather.10.cloned.1.call-update) | async-done | bytes 1179664 | tf_op jit(solution)/shard_map/all_gather | solution.py:210
  83.5 21.7 all-gather.18.cloned.1.call-done
  107.0 25.3 %all-gather.16.cloned.1.call-done = bf16[1024,768]{1,0:T(8,128)(2,1)} async-done(((bf16[128,768]{1,0:T(8,128)(2,1)}), bf16[1024,768]{1,0:T(8,128)(2,1)}) %all-gather.16.cloned.1.call-update) | async-done | bytes 1572880 | tf_op jit(solution)/shard_map/all_gather | solution.py:228
  134.9 241.1 %while.43 = (s32[]{:T(128)}, f32[12,128]{1,0:T(8,128)S(1)}, f32[12,128]{1,0:T(8,128)S(1)}, s32[]{:T(128)}, bf16[1024,12,64]{0,2,1:T(8,128)(2,1)}, /*index=5*/bf1...) while((s32[]{:T(128)}, f32[12,128]{1,0:T(8,128)S(1)}, ...), condition=%wide.region_4.6_spmd.clone, body=%wide.region_1.5_spmd.clone.sunk | while | flops 107155080 | bytes 25188016 | solution.py:87
  135.2 217.0 %gather_fusion = f32[65536,12]{1,0:T(8,128)} fusion(f32[12,1024]{0,1:T(8,128)S(1)} %get-tuple-element.903, s32[65536]{0:T(1024)S(1)} %broadcast_clamp_fusion.6), kind=kCustom, calls=%fused_computation.clone.clone.1 | custom fusion | bytes 6553600 | tf_op jit(solution)/shard_map/while/body/jit(_take)/gather | solution.py:36
  352.2 19.5 copy.200
  372.3 3.2 fusion.198
  378.7 244.3 %while.44 = (s32[]{:T(128)}, f32[128,12,64]{0,2,1:T(8,128)S(1)}, f32[128,12,64]{0,2,1:T(8,128)S(1)}, s32[]{:T(128)}, bf16[1024,12,64]{0,2,1:T(8,128)(2,1)}, /*in...) while((s32[]{:T(128)}, f32[128,12,64]{0,2,1:T(8,128)S(1)}, ...), condition=%wide.region_6.8_spmd.clone, body=%wide.region_5.7_spmd.clone.sunk | while | flops 311034496 | bytes 31405768 | solution.py:107
  379.0 217.0 %gather_fusion.1 = f32[65536,12]{1,0:T(8,128)} fusion(f32[12,1024]{0,1:T(8,128)S(1)} %get-tuple-element.944, s32[65536]{0:T(1024)S(1)} %broadcast_clamp_fusion.7), kind=kCustom, calls=%fused_computation.2.clone.clone.1 | custom fusion | bytes 6553600 | tf_op jit(solution)/shard_map/while/body/jit(_take)/gather | solution.py:36
  596.0 19.5 copy.204
  616.1 3.4 fusion.205
  629.3 487.9 %all-to-all-start = ((bf16[8,36,768]{2,1,0:T(8,128)(2,1)}), bf16[8,36,768]{2,1,0:T(8,128)(2,1)S(1)}, u32[]{:S(2)}, u32[]{:S(2)}) async-start(bf16[8,36,768]{2,1,0:T(8,128)(2,1)} %reshape.396), calls=%async_computation | async-start | bytes 983040 | tf_op jit(solution)/shard_map/all_to_all | solution.py:260
  1120.0 13.2 all-gather
  1133.8 5.3 fusion.74
  1141.0 9.8 multiply_convert_fusion
  1150.8 5.5 fusion.70
  1156.3 4.3 all-to-all-start.1
  1160.6 9.4 all-to-all-done.1
  1178.1 3.5 all-to-all-start.2
  1181.8 9.2 all-to-all-done.2
  1191.0 7.6 add_convert_fusion
  1199.8 4.9 fusion.67
  1204.7 4.3 all-to-all-start.3
  1209.1 9.3 all-to-all-done.3
  1233.4 3.4 broadcast_in_dim.139
  1236.9 285.4 %while.45 = (s32[]{:T(128)}, f32[128,12,64]{0,2,1:T(8,128)S(1)}, f32[12,1792]{1,0:T(8,128)S(1)}, f32[1024,1536]{0,1:T(8,128)}, s32[]{:T(128)}, /*index=5*/bf16[1...) while((s32[]{:T(128)}, f32[128,12,64]{0,2,1:T(8,128)S(1)}, ...), condition=%wide.region_27.30_spmd.clone, body=%wide.region_25.29_spmd.clone.sunk | while | flops 513637504 | bytes 102934064 | solution.py:167
  1237.4 217.0 %gather_fusion.2 = f32[65536,12]{1,0:T(8,128)} fusion(f32[12,1024]{0,1:T(8,128)S(1)} %get-tuple-element.1000, s32[65536]{0:T(1024)S(1)} %broadcast_clamp_fusion.8), kind=kCustom, calls=%fused_computation.3.clone.clone.1 | custom fusion | bytes 6553600 | tf_op jit(solution)/shard_map/while/body/jit(_take)/gather | solution.py:36
  1454.4 19.4 copy.208
  1474.4 3.4 fusion.219
  1483.1 15.4 rev.8
  1498.5 3.6 copy.211
  1510.5 6.9 reshape.525
  1529.1 339.7 %reduce-scatter.13.cloned.1.call-done = f32[128,1536]{0,1:T(8,128)} async-done(((f32[1024,1536]{0,1:T(8,128)}), f32[128,1536]{0,1:T(8,128)}) %reduce-scatter.13.cloned.1.call-update) | async-done | bytes 786448 | tf_op jit(solution)/shard_map/reduce_scatter | solution.py:343
  1874.2 5.4 fusion.58
  1879.6 20.3 copy.175
  1899.8 7.7 copy.184
  1909.2 4.4 fusion.57
  1919.1 22.5 reduce-scatter.15.cloned.1.call-done
  1941.6 49.7 %reduce-scatter.21.cloned.1.call-done = f32[192,768]{1,0:T(8,128)} async-done(((f32[768,768]{1,0:T(8,128)}), f32[192,768]{1,0:T(8,128)}) %reduce-scatter.21.cloned.1.call-update) | async-done | bytes 589840 | tf_op jit(solution)/shard_map/reduce_scatter | solution.py:368
  1991.3 50.4 %reduce-scatter.17.cloned.1.call-done = f32[192,768]{1,0:T(8,128)} async-done(((f32[768,768]{1,0:T(8,128)}), f32[192,768]{1,0:T(8,128)}) %reduce-scatter.17.cloned.1.call-update) | async-done | bytes 589840 | tf_op jit(solution)/shard_map/reduce_scatter | solution.py:366
  2041.7 49.7 %reduce-scatter.19.cloned.1.call-done = f32[192,768]{1,0:T(8,128)} async-done(((f32[768,768]{1,0:T(8,128)}), f32[192,768]{1,0:T(8,128)}) %reduce-scatter.19.cloned.1.call-update) | async-done | bytes 589840 | tf_op jit(solution)/shard_map/reduce_scatter | solution.py:367
  2091.5 86.9 %reduce-scatter.27.cloned.1.call-done = bf16[192,3072]{1,0:T(8,128)(2,1)} async-done(((bf16[768,3072]{1,0:T(8,128)(2,1)}), bf16[192,3072]{1,0:T(8,128)(2,1)}) %reduce-scatter.27.cloned.1.call-update) | async-done | bytes 1179664
  2180.9 3.9 copy.176
  2187.8 78.5 %reduce-scatter.23.cloned.1.call-done = bf16[1,192,3072]{2,1,0:T(8,128)(2,1)} async-done(((bf16[1,768,3072]{2,1,0:T(8,128)(2,1)}), bf16[1,192,3072]{2,1,0:T(8,128)(2,1)}) %reduce-scatter.23.cloned.1.call-update) | async-done | bytes 1179664 | tf_op jit(solution)/shard_map/reduce_scatter | solution.py:306
  2272.6 18.2 all-reduce.6
  2290.9 23.1 all-reduce.4
  2314.9 18.7 all-reduce.9.cloned.1.call-done
  (319 shorter events, 120.3 us)
Async XLA Ops:
  7.2 72.2 %copy-start = (f32[32,12]{0,1:T(8,128)S(1)}, f32[32,12]{0,1:T(8,128)}, u32[]{:S(2)}) copy-start(f32[32,12]{0,1:T(8,128)} %param.32) | copy-start | bytes 4612
  7.2 71.3 %copy-start.46 = (s32[1,128,2]{1,2,0:T(2,128)S(1)}, s32[1,128,2]{1,2,0:T(2,128)}, u32[]{:S(2)}) copy-start(s32[1,128,2]{1,2,0:T(2,128)} %param.38) | copy-start | bytes 3076
  7.2 71.7 %copy-start.42 = (s32[1,128,2]{1,2,0:T(2,128)S(1)}, s32[1,128,2]{1,2,0:T(2,128)}, u32[]{:S(2)}) copy-start(s32[1,128,2]{1,2,0:T(2,128)} %param.37) | copy-start | bytes 3076
  7.2 72.2 %copy-start.57 = (s32[1024]{0:T(1024)S(1)}, s32[1024]{0:T(1024)}, u32[]{:S(2)}) copy-start(s32[1024]{0:T(1024)} %param.39) | copy-start | bytes 12292
  7.2 35.6 %all-gather.14.cloned.1.call-start = ((), (), s32[]{:S(2)}) async-start(), calls=%async_computation.14 | async-start | bytes 1474560 | tf_op jit(solution)/shard_map/all_gather | solution.py:209
  8.0 66.0 %all-gather.10.cloned.1.call-start = ((), (), s32[]{:S(2)}) async-start(), calls=%async_computation.12 | async-start | bytes 1474560 | tf_op jit(solution)/shard_map/all_gather | solution.py:210
  8.7 96.5 %all-gather.18.cloned.1.call-start = ((), (), s32[]{:S(2)}) async-start(), calls=%async_computation.16 | async-start | bytes 1474560 | tf_op jit(solution)/shard_map/all_gather | solution.py:208
  9.4 72.7 %copy-start.21 = (bf16[1,128,768]{2,1,0:T(8,128)(2,1)S(1)}, bf16[1,128,768]{2,1,0:T(8,128)(2,1)}, u32[]{:S(2)}) copy-start(bf16[1,128,768]{2,1,0:T(8,128)(2,1)} %param.26) | copy-start | bytes 589828
  9.5 122.9 %all-gather.16.cloned.1.call-start = ((), (), s32[]{:S(2)}) async-start(), calls=%async_computation.15 | async-start | bytes 1769472 | tf_op jit(solution)/shard_map/all_gather | solution.py:228
  11.2 94.1 %copy-start.35 = (f32[128]{0:T(128)}, f32[128]{0:T(128)S(1)}, u32[]{:S(2)}) copy-start(f32[128]{0:T(128)S(1)} %fusion.127) | copy-start | bytes 1540
  11.2 94.1 %copy-start.2 = (bf16[1,128,768]{2,1,0:T(8,128)(2,1)S(1)}, bf16[1,128,768]{2,1,0:T(8,128)(2,1)}, u32[]{:S(2)}) copy-start(bf16[1,128,768]{2,1,0:T(8,128)(2,1)} %param.25) | copy-start | bytes 589828
  11.2 94.1 %copy-start.27 = (f32[768]{0:T(1024)S(1)}, f32[768]{0:T(1024)}, u32[]{:S(2)}) copy-start(f32[768]{0:T(1024)} %param.27) | copy-start | bytes 9220
  45.3 330.8 %all-gather.12.cloned.1.call-start = ((), (), s32[]{:S(2)}) async-start(), calls=%async_computation.13 | async-start | bytes 1769472 | tf_op jit(solution)/shard_map/all_gather | solution.py:229
  76.4 546.7 %all-gather.20.cloned.1.call-start = ((), (), s32[]{:S(2)}) async-start(), calls=%async_computation.17 | async-start | bytes 1474560 | tf_op jit(solution)/shard_map/all_gather | solution.py:211
  77.0 1056.8 %all-gather.22.cloned.1.call-start = ((), (), s32[]{:S(2)}) async-start(), calls=%async_computation.18 | async-start | bytes 5898240 | tf_op jit(solution)/shard_map/all_gather | solution.py:213
  77.8 1073.0 %all-gather.24.cloned.1.call-start = ((), (), s32[]{:S(2)}) async-start(), calls=%async_computation.19 | async-start | bytes 5898240 | tf_op jit(solution)/shard_map/all_gather | solution.py:214
  78.9 56.0 %copy-start.40 = (s32[256]{0:T(256)}, s32[256]{0:T(256)S(1)}, u32[]{:S(2)}) copy-start(s32[256]{0:T(256)S(1)} %mul.375) | copy-start | bytes 3076
  378.7 244.4 %copy-start.3 = (bf16[1,128,768]{2,1,0:T(8,128)(2,1)S(1)}, bf16[1,128,768]{2,1,0:T(8,128)(2,1)}, u32[]{:S(2)}) copy-start(bf16[1,128,768]{2,1,0:T(8,128)(2,1)} %param.25) | copy-start | bytes 589828
  378.7 246.3 %copy-start.31 = (f32[768]{0:T(1024)S(1)}, f32[768]{0:T(1024)}, u32[]{:S(2)}) copy-start(f32[768]{0:T(1024)} %param.33) | copy-start | bytes 9220
  623.0 494.1 %copy-start.52 = (s32[256]{0:T(256)S(1)}, s32[256]{0:T(256)}, u32[]{:S(2)}) copy-start(s32[256]{0:T(256)} %get-tuple-element.636) | copy-start | bytes 3076
  623.0 494.1 %copy-start.18 = (f32[128,768]{1,0:T(8,128)S(1)}, f32[128,768]{1,0:T(8,128)}, u32[]{:S(2)}) copy-start(f32[128,768]{1,0:T(8,128)} %bitcast_convert_fusion.2) | copy-start | bytes 1179652
  624.9 605.5 %copy-start.5 = (f32[128,768]{1,0:T(8,128)}, f32[128,768]{1,0:T(8,128)S(1)}, u32[]{:S(2)}) copy-start(f32[128,768]{1,0:T(8,128)S(1)} %get-tuple-element.653) | copy-start | bytes 1179652
  624.9 495.1 %copy-start.51 = (bf16[192,8]{0,1:T(8,128)(2,1)S(1)}, bf16[192,8]{0,1:T(8,128)(2,1)}, u32[]{:S(2)}) copy-start(bf16[192,8]{0,1:T(8,128)(2,1)} %param.34) | copy-start | bytes 9220
  625.0 605.5 %copy-start.44 = (f32[128]{0:T(128)}, f32[128]{0:T(128)S(1)}, u32[]{:S(2)}) copy-start(f32[128]{0:T(128)S(1)} %fusion.128) | copy-start | bytes 1540
  629.3 504.5 %all-to-all-start = ((bf16[8,36,768]{2,1,0:T(8,128)(2,1)}), bf16[8,36,768]{2,1,0:T(8,128)(2,1)S(1)}, u32[]{:S(2)}, u32[]{:S(2)}) async-start(bf16[8,36,768]{2,1,0:T(8,128)(2,1)} %reshape.396), calls=%async_computation | async-start | bytes 983040 | tf_op jit(solution)/shard_map/all_to_all | solution.py:260
  1133.7 94.6 %copy-start.29 = (f32[128,8]{0,1:T(8,128)}, f32[128,8]{0,1:T(8,128)S(1)}, u32[]{:S(2)}) copy-start(f32[128,8]{0,1:T(8,128)S(1)} %get-tuple-element.656) | copy-start | bytes 12292
  1133.7 94.6 %copy-start.37 = (f32[128]{0:T(128)}, f32[128]{0:T(128)S(1)}, u32[]{:S(2)}) copy-start(f32[128]{0:T(128)S(1)} %get-tuple-element.655) | copy-start | bytes 1540
  1133.8 94.6 %copy-start.48 = (f32[128]{0:T(128)}, f32[128]{0:T(128)S(1)}, u32[]{:S(2)}) copy-start(f32[128]{0:T(128)S(1)} %fusion.126) | copy-start | bytes 1540
  1156.3 18.6 copy-start.41
  1156.3 13.8 all-to-all-start.1
  1178.1 12.8 all-to-all-start.2
  1204.7 13.7 all-to-all-start.3
  1209.0 659.9 %reduce-scatter.13.cloned.1.call-start = ((), (), s32[]{:S(2)}) async-start(), calls=%async_computation.20 | async-start | bytes 7077888 | tf_op jit(solution)/shard_map/reduce_scatter | solution.py:343
  1209.1 19.3 copy-start.33
  1209.1 19.2 copy-start.53
  1523.0 393.2 %reduce-scatter.25.cloned.1.call-start = ((), (), s32[]{:S(2)}) async-start(), calls=%async_computation.26 | async-start | bytes 491520
  1525.0 416.5 %reduce-scatter.15.cloned.1.call-start = ((), (), s32[]{:S(2)}) async-start(), calls=%async_computation.21 | async-start | bytes 2949120 | tf_op jit(solution)/shard_map/reduce_scatter | solution.py:365
  1527.2 464.1 %reduce-scatter.21.cloned.1.call-start = ((), (), s32[]{:S(2)}) async-start(), calls=%async_computation.24 | async-start | bytes 2949120 | tf_op jit(solution)/shard_map/reduce_scatter | solution.py:368
  1529.1 512.6 %reduce-scatter.17.cloned.1.call-start = ((), (), s32[]{:S(2)}) async-start(), calls=%async_computation.22 | async-start | bytes 2949120 | tf_op jit(solution)/shard_map/reduce_scatter | solution.py:366
  1872.1 219.4 %reduce-scatter.19.cloned.1.call-start = ((), (), s32[]{:S(2)}) async-start(), calls=%async_computation.23 | async-start | bytes 2949120 | tf_op jit(solution)/shard_map/reduce_scatter | solution.py:367
  1874.1 304.2 %reduce-scatter.27.cloned.1.call-start = ((), (), s32[]{:S(2)}) async-start(), calls=%async_computation.27 | async-start | bytes 5898240
  1907.5 358.8 %reduce-scatter.23.cloned.1.call-start = ((), (), s32[]{:S(2)}) async-start(), calls=%async_computation.25 | async-start | bytes 5898240 | tf_op jit(solution)/shard_map/reduce_scatter | solution.py:306
  1913.7 420.0 %all-reduce.9.cloned.1.call-start = ((), (), s32[]{:S(2)}) async-start(), calls=%async_computation.28 | async-start | bytes 4718592 | tf_op jit(solution)/shard_map/psum | solution.py:374
  2184.8 84.5 %copy-start.9 = (bf16[768,768]{1,0:T(8,128)(2,1)S(1)}, bf16[768,768]{1,0:T(8,128)(2,1)}, u32[]{:S(2)}) copy-start(bf16[768,768]{1,0:T(8,128)(2,1)} %all-gather.14.cloned.1.call-done) | copy-start | bytes 3538948
  2184.8 86.2 %copy-start.10 = (bf16[768,768]{1,0:T(8,128)(2,1)S(1)}, bf16[768,768]{1,0:T(8,128)(2,1)}, u32[]{:S(2)}) copy-start(bf16[768,768]{1,0:T(8,128)(2,1)} %all-gather.10.cloned.1.call-done) | copy-start | bytes 3538948
  2187.8 84.8 %copy-start.39 = (f32[768]{0:T(1024)S(1)}, f32[768]{0:T(1024)}, u32[]{:S(2)}) copy-start(f32[768]{0:T(1024)} %get-tuple-element.552) | copy-start | bytes 9220
  2187.8 126.2 %copy-start.56 = (f32[128]{0:T(128)S(1)}, f32[128]{0:T(128)}, u32[]{:S(2)}) copy-start(f32[128]{0:T(128)} %copy-done.55) | copy-start | bytes 1540
  2269.3 71.0 %copy-start.1 = (f32[32,12]{0,1:T(8,128)S(1)}, f32[32,12]{0,1:T(8,128)}, u32[]{:S(2)}) copy-start(f32[32,12]{0,1:T(8,128)} %param.32) | copy-start | bytes 4612
  (35 other events, 146.8 us)
Sparse Core Ops, SparseCore 0:
  9.6 33.1 all-gather.13
  44.4 29.5 all-gather.9
  75.5 29.6 all-gather.17
  107.5 24.7 all-gather.15
  134.6 25.6 all-gather.11
  161.8 30.4 all-gather.19
  193.8 88.5 all-gather.21
  284.0 87.8 all-gather.23
  1523.1 345.7 reduce-scatter.12
  1871.7 20.5 reduce-scatter.24
  1895.2 46.3 reduce-scatter.14
  1943.7 47.5 reduce-scatter.20
  1994.2 47.5 reduce-scatter.16
  2043.9 47.5 reduce-scatter.18
  2093.6 84.7 reduce-scatter.26
  2180.5 85.7 reduce-scatter.22
  2269.7 63.9 all-reduce.8
where the time goes:
time: 2360 us; the launch traced here: 2350 us
  waiting for transfers between devices  836 us (35%)
  local copies, waits for them, and re-layouts  827 us (35%)
  starting transfers between devices  501 us (21%)
  matrix products  77.8 us (3%)
  blocking collectives  54.5 us (2%)
  other arithmetic  33.9 us (1%)
    gather x6, local copies, waits for them, and re-layouts, block_scores(): bias_values = jnp.take(offset_bias, clipped, axis=1)  709 us
    all_to_all x1, starting transfers between devices, on_device(): lax.all_to_all(outgoing, 'expert', split_axis=0, concat_axis=0, tiled=True)  488 us
    reduce_scatter x1, waiting for transfers between devices, on_device(): lax.psum_scatter(partial_sums, 'expert', scatter_dimension=0, tiled=True)  340 us
    unnamed x19, waiting for transfers between devices  91.1 us
    reduce_scatter x1, waiting for transfers between devices, on_device(): lax.psum_scatter(grad_first[None].astype(jnp.bfloat16), 'dp', scatter_dim...  78.5 us
    unnamed x142, local copies, waits for them, and re-layouts  53.3 us
    reduce_scatter x1, waiting for transfers between devices, on_device(): lax.psum_scatter(grad_key_w, 'dp', scatter_dimension=0, tiled=True)  50.4 us
    reduce_scatter x1, waiting for transfers between devices, on_device(): lax.psum_scatter(grad_value_w, 'dp', scatter_dimension=0, tiled=True)  49.7 us
  transfers between devices with their start and end apart: 21, of which 15 were waited for; matrix products, arithmetic and copies ran while one was open for 25% of the time, Pallas kernels for 0%

commit v1 on v0

v1 whole, which is shorter than its diff:
```python
from functools import partial

import jax
import jax.numpy as jnp
from jax import lax
from jax.experimental import pallas as pl
from jax.experimental.pallas import tpu as pltpu
from jax.sharding import PartitionSpec as P

HIGHEST = lax.Precision.HIGHEST
NEGATIVE = -1e30
EPSILON = 1e-06
LANES = 128
VMEM_BYTES = 56 * 1024 * 1024


def rms_norm(values, scale_gain):
    return (
        values * lax.rsqrt(jnp.mean(values * values, axis=-1, keepdims=True) + EPSILON) * scale_gain
    )


def dot_nt(left, right):
    return lax.dot_general(
        left, right, (((1,), (1,)), ((), ())), preferred_element_type=jnp.float32
    )


def dot_nn(left, right):
    return jnp.dot(left, right, preferred_element_type=jnp.float32)


def spread_diagonals(row, rows, cols):
    wide = jnp.broadcast_to(row, (rows, row.shape[1]))
    return pltpu.roll(wide, 0, 1, stride=1, stride_axis=0)[:, :cols]


def head_masks(half):
    lane = lax.broadcasted_iota(jnp.int32, (1, LANES), 1)
    first = lane < half
    return (first, (first.astype(jnp.bfloat16), 1 - first.astype(jnp.bfloat16)))


def attend_kernel(q_ref, k_ref, v_ref, line_ref, mixed_ref, exact_ref, log_ref):
    half = LANES // 2
    first, masks = head_masks(half)
    rows, seq_len = (q_ref.shape[0], k_ref.shape[0])
    queries, keys, values = (q_ref[...], k_ref[...], v_ref[...])
    outs = []
    for head in range(2):
        scores = dot_nt(queries * masks[head], keys) * 0.125
        scores = scores + spread_diagonals(line_ref[head : head + 1, :], rows, seq_len)
        top = jnp.max(scores, axis=1, keepdims=True)
        raised = jnp.exp(scores - top)
        total = jnp.sum(raised, axis=1, keepdims=True)
        weights = raised * (1.0 / total)
        upper = weights.astype(jnp.bfloat16)
        lower = (weights - upper.astype(jnp.float32)).astype(jnp.bfloat16)
        rounded = dot_nn(upper, values)
        outs.append((rounded, rounded + dot_nn(lower, values), top + jnp.log(total)))
    mixed_ref[...] = jnp.where(first, outs[0][0], outs[1][0]).astype(jnp.bfloat16)
    exact_ref[...] = jnp.where(first, outs[0][1], outs[1][1])
    log_ref[...] = jnp.where(first, outs[0][2], outs[1][2])


def query_grad_kernel(q_ref, k_ref, v_ref, line_ref, grad_ref, exact_ref, log_ref, dq_ref, diag_ref):
    half = LANES // 2
    first, masks = head_masks(half)
    rows, seq_len = (q_ref.shape[0], k_ref.shape[0])
    queries, keys, values, grads = (q_ref[...], k_ref[...], v_ref[...], grad_ref[...])
    products = grads.astype(jnp.float32) * exact_ref[...]
    flip = (
        lax.broadcasted_iota(jnp.int32, (rows, rows), 0)
        + lax.broadcasted_iota(jnp.int32, (rows, rows), 1)
        == rows - 1
    ).astype(jnp.bfloat16)
    outs = []
    for head in range(2):
        scores = dot_nt(queries * masks[head], keys) * 0.125
        scores = scores + spread_diagonals(line_ref[head : head + 1, :], rows, seq_len)
        place = head * half
        weights = jnp.exp(scores - log_ref[:, place : place + 1])
        row_dots = jnp.sum(
            jnp.where(first if head == 0 else ~first, products, 0.0), axis=1, keepdims=True
        )
        grad_weights = dot_nt(grads * masks[head], values)
        grad_scores = (weights * (grad_weights - row_dots)).astype(jnp.bfloat16)
        outs.append(dot_nn(grad_scores, keys) * 0.125)
        turned = jnp.concatenate(
            [dot_nn(flip, grad_scores), jnp.zeros((rows, rows), jnp.float32)], axis=1
        )
        lined = pltpu.roll(turned, 0, 1, stride=1, stride_axis=0)
        diag_ref[head : head + 1, :] = jnp.sum(lined, axis=0, keepdims=True)
    dq_ref[...] = jnp.where(first, outs[0], outs[1]).astype(jnp.bfloat16)


def key_grad_kernel(k_ref, v_ref, q_ref, grad_ref, line_ref, stat_ref, dk_ref, dv_ref):
    half = LANES // 2
    first, masks = head_masks(half)
    rows, seq_len = (k_ref.shape[0], q_ref.shape[0])
    queries, keys, values, grads = (q_ref[...], k_ref[...], v_ref[...], grad_ref[...])
    outs = []
    for head in range(2):
        scores = dot_nt(keys * masks[head], queries) * 0.125
        scores = scores + spread_diagonals(line_ref[head : head + 1, :], rows, seq_len)
        weights = jnp.exp(scores - stat_ref[head : head + 1, :])
        grad_weights = dot_nt(values * masks[head], grads)
        grad_scores = (weights * (grad_weights - stat_ref[2 + head : 3 + head, :])).astype(
            jnp.bfloat16
        )
        outs.append(
            (dot_nn(grad_scores, queries) * 0.125, dot_nn(weights.astype(jnp.bfloat16), grads))
        )
    dk_ref[...] = jnp.where(first, outs[0][0], outs[1][0]).astype(jnp.bfloat16)
    dv_ref[...] = jnp.where(first, outs[0][1], outs[1][1]).astype(jnp.bfloat16)


def columns(rows, shift):
    return pl.BlockSpec((rows, LANES), lambda pair: (0, pair + shift))


def planes(depth, width):
    return pl.BlockSpec((None, depth, width), lambda pair: (pair, 0, 0))


def pair_call(kernel, pairs, in_specs, out_specs, out_shape, cost):
    return pl.pallas_call(
        kernel,
        grid=(pairs,),
        in_specs=in_specs,
        out_specs=out_specs,
        out_shape=out_shape,
        cost_estimate=pl.CostEstimate(flops=cost, bytes_accessed=cost // 100, transcendentals=0),
        compiler_params=pltpu.CompilerParams(vmem_limit_bytes=VMEM_BYTES),
    )


def split_three(values):
    top = lax.reduce_precision(values, 8, 7)
    rest = values - top
    middle = lax.reduce_precision(rest, 8, 7)
    return jnp.concatenate([top, middle, rest - middle], axis=1).astype(jnp.bfloat16)


def on_device(
    hidden,
    cotangent,
    norm1_gain,
    w_query,
    w_key,
    w_value,
    w_output,
    bias_table,
    norm2_gain,
    w_router,
    w_in,
    w_out,
    expert_ids,
    keep_mask,
    buckets,
):
    tok_rows = hidden.shape[1]
    model_width = hidden.shape[2]
    head_count = bias_table.shape[1]
    head_size = model_width // head_count
    experts = w_router.shape[1]
    capacity = 9 * tok_rows // (4 * experts)
    seq_len = buckets.shape[0]
    pairs = model_width // LANES
    bucket_count = bias_table.shape[0]
    my_index = lax.axis_index("expert")
    query_start = my_index * tok_rows
    width = seq_len + tok_rows

    wqkv = jnp.concatenate([w_query, w_key, w_value], axis=1)
    wrest = jnp.concatenate(
        [w_output, jnp.pad(w_router, ((0, 0), (0, LANES - experts)))], axis=1
    )
    wqkv_all = lax.all_gather(wqkv, "dp", axis=0, tiled=True)
    wrest_all = lax.all_gather(wrest, "dp", axis=0, tiled=True)
    first_weight = lax.all_gather(w_in[0], "dp", axis=0, tiled=True)
    second_turned = lax.all_gather(w_out[0].T, "dp", axis=0, tiled=True)
    output_all = wrest_all[:, :model_width]
    router = wrest_all[:, model_width : model_width + experts].astype(jnp.float32)

    def filler(count):
        return jnp.full((count,), bucket_count, jnp.int32)

    falling = jnp.concatenate([filler(tok_rows + 1), buckets[::-1], filler(seq_len)])
    rising = jnp.concatenate([filler(seq_len), buckets, filler(tok_rows)])
    seen = lax.dynamic_slice_in_dim(falling, seq_len - query_start, width, 0)
    seen_sums = lax.dynamic_slice_in_dim(falling, seq_len - query_start + 1, width, 0)
    seen_turned = lax.dynamic_slice_in_dim(
        rising, seq_len - tok_rows - query_start, width, 0
    )

    def bias_line(numbers):
        turned = jnp.concatenate([numbers[tok_rows:], numbers[:tok_rows]])
        onehot = (
            jnp.arange(bucket_count, dtype=jnp.int32)[:, None] == turned[None, :]
        ).astype(jnp.float32)
        line = lax.dot_general(
            bias_table, onehot, (((0,), (0,)), ((), ())), precision=HIGHEST
        )
        line = jnp.where((turned < bucket_count)[None, :], line, NEGATIVE)
        return line.reshape(pairs, 2, width)

    line = bias_line(seen)
    line_turned = bias_line(seen_turned)

    inputs = hidden[0].astype(jnp.float32)
    normed1_f, norm1_back = jax.vjp(rms_norm, inputs, norm1_gain)
    normed1 = normed1_f.astype(jnp.bfloat16)
    projected = jnp.dot(normed1, wqkv_all, preferred_element_type=jnp.float32).astype(jnp.bfloat16)
    mixed_all = lax.all_gather(projected, "expert", axis=0, tiled=True)
    pair_cost = 2 * tok_rows * seq_len * model_width
    mixer_specs = [
        columns(tok_rows, 0),
        columns(seq_len, pairs),
        columns(seq_len, 2 * pairs),
        planes(2, width),
    ]
    wide_shape = jax.ShapeDtypeStruct((tok_rows, model_width), jnp.float32)
    low_shape = jax.ShapeDtypeStruct((tok_rows, model_width), jnp.bfloat16)
    attended, exact_out, log_wide = pair_call(
        attend_kernel,
        pairs,
        mixer_specs,
        [columns(tok_rows, 0)] * 3,
        [low_shape, wide_shape, wide_shape],
        3 * pair_cost,
    )(projected, mixed_all, mixed_all, line)
    resid = inputs + jnp.dot(attended, output_all, preferred_element_type=jnp.float32)
    chosen = (
        expert_ids[0][:, :, None] == jnp.arange(experts, dtype=jnp.int32)[None, None, :]
    ).astype(jnp.float32)
    kept = keep_mask[0].astype(jnp.float32)

    def route(resid_rows, gain_two, router_weight):
        normed = rms_norm(resid_rows, gain_two)
        probs = jax.nn.softmax(jnp.dot(normed, router_weight, precision=HIGHEST), axis=-1)
        picked = jnp.sum(probs[:, None, :] * chosen, axis=-1)
        return (normed, picked / jnp.sum(picked, axis=-1, keepdims=True) * kept)

    (normed2_f, gates), route_back = jax.vjp(route, resid, norm2_gain, router)
    normed2 = normed2_f.astype(jnp.bfloat16)
    grad_top = cotangent[0].astype(jnp.float32)
    grad_made = (gates[:, :, None] * grad_top[:, None, :]).astype(jnp.bfloat16)
    markers = chosen * kept[:, :, None]
    both = markers.reshape(tok_rows, 2 * experts).astype(jnp.bfloat16)
    row_number = jnp.arange(tok_rows, dtype=jnp.int32)
    before = (row_number[None, :] < row_number[:, None]).astype(jnp.bfloat16)
    counts = jnp.dot(before, both, preferred_element_type=jnp.float32).reshape(
        tok_rows, 2, experts
    )
    counts = counts + jnp.stack(
        [jnp.zeros((experts,), jnp.float32), jnp.sum(markers[:, 0, :], axis=0)]
    )
    places = jnp.sum(counts * markers, axis=-1).astype(jnp.int32)
    slots = experts * capacity
    targets = jnp.where(
        keep_mask[0] > 0, expert_ids[0] * capacity + places, slots
    )
    flat_targets = jnp.concatenate([targets[:, 0], targets[:, 1]])
    placing = (
        flat_targets[:, None] == jnp.arange(slots, dtype=jnp.int32)[None, :]
    ).astype(jnp.bfloat16)
    rows_out = jnp.concatenate(
        [
            jnp.concatenate([normed2, grad_made[:, 0]], axis=1),
            jnp.concatenate([normed2, grad_made[:, 1]], axis=1),
        ],
        axis=0,
    )
    outgoing = (
        lax.dot_general(
            placing, rows_out, (((0,), (0,)), ((), ())), preferred_element_type=jnp.float32
        )
        .astype(jnp.bfloat16)
        .reshape(experts, capacity, 2 * model_width)
    )
    received = lax.all_to_all(
        outgoing, "expert", split_axis=0, concat_axis=0, tiled=True
    ).reshape(slots, 2 * model_width)
    arrived = received[:, :model_width]
    grad_arrived = received[:, model_width:]
    pre_act = jnp.dot(arrived, first_weight, preferred_element_type=jnp.float32)
    normal_cdf = 0.5 * (1.0 + lax.erf(pre_act * (0.5**0.5)))
    activated = (pre_act * normal_cdf).astype(jnp.bfloat16)
    slope = normal_cdf + pre_act * (jnp.exp(-0.5 * pre_act * pre_act) * 0.3989422804014327)
    expert_out = dot_nt(activated, second_turned).astype(jnp.bfloat16)
    grad_act = jnp.dot(grad_arrived, second_turned, preferred_element_type=jnp.float32)
    grad_pre = (grad_act * slope).astype(jnp.bfloat16)
    grad_rows = dot_nt(grad_pre, first_weight).astype(jnp.bfloat16)
    returned = lax.all_to_all(
        jnp.concatenate([expert_out, grad_rows], axis=1).reshape(
            experts, capacity, 2 * model_width
        ),
        "expert",
        split_axis=0,
        concat_axis=0,
        tiled=True,
    ).reshape(slots, 2 * model_width)

    def outer(left, right):
        return lax.dot_general(
            left, right, (((0,), (0,)), ((), ())), preferred_element_type=jnp.float32
        )

    grad_first = outer(arrived, grad_pre).astype(jnp.bfloat16)
    grad_second = outer(grad_arrived, activated).astype(jnp.bfloat16)
    first_sum = lax.psum_scatter(grad_first, "dp", scatter_dimension=0, tiled=True)
    second_sum = lax.psum_scatter(grad_second, "dp", scatter_dimension=0, tiled=True)
    back = jnp.dot(placing, returned, preferred_element_type=jnp.float32).reshape(
        2, tok_rows, 2 * model_width
    )
    picked_rows = jnp.transpose(back[:, :, :model_width], (1, 0, 2))
    output = (resid + jnp.sum(gates[:, :, None] * picked_rows, axis=1)).astype(jnp.bfloat16)
    grad_gates = jnp.sum(picked_rows * grad_top[:, None, :], axis=-1)
    grad_normed2 = back[0, :, model_width:] + back[1, :, model_width:]
    grad_resid_norm, grad_gain_two, grad_router = route_back((grad_normed2, grad_gates))
    grad_resid = grad_top + grad_resid_norm
    grad_branch = grad_resid.astype(jnp.bfloat16)
    grad_attended = dot_nt(grad_branch, output_all).astype(jnp.bfloat16)
    row_dots = jnp.sum(
        (grad_attended.astype(jnp.float32) * exact_out).reshape(tok_rows, head_count, head_size),
        axis=2,
    )
    log_total = log_wide.reshape(tok_rows, head_count, head_size)[:, :, 0]
    stats = jnp.concatenate([split_three(log_total), split_three(row_dots)], axis=1)
    stats = jnp.pad(stats, ((0, 0), (0, LANES - stats.shape[1])))
    packed = jnp.concatenate([grad_attended, stats], axis=1)
    packed_all = lax.all_gather(packed, "expert", axis=0, tiled=True)
    grad_query_low, diagonals = pair_call(
        query_grad_kernel,
        pairs,
        mixer_specs + [columns(tok_rows, 0)] * 3,
        [columns(tok_rows, 0), planes(2, width)],
        [low_shape, jax.ShapeDtypeStruct((pairs, 2, width), jnp.float32)],
        5 * pair_cost,
    )(projected, mixed_all, mixed_all, line, grad_attended, exact_out, log_wide)
    grad_output = outer(attended, grad_branch).astype(jnp.bfloat16)
    output_sum = lax.psum_scatter(grad_output, "dp", scatter_dimension=0, tiled=True)
    stats_all = packed_all[:, model_width : model_width + 6 * head_count].astype(jnp.float32)
    stats_all = jnp.sum(stats_all.reshape(seq_len, 2, 3, pairs, 2), axis=2)
    stats_all = jnp.transpose(stats_all, (2, 1, 3, 0)).reshape(pairs, 4, seq_len)
    grad_keys, grad_values = pair_call(
        key_grad_kernel,
        pairs,
        [
            columns(tok_rows, pairs),
            columns(tok_rows, 2 * pairs),
            columns(seq_len, 0),
            columns(seq_len, 0),
            planes(2, width),
            planes(4, seq_len),
        ],
        [columns(tok_rows, 0)] * 2,
        [low_shape, low_shape],
        4 * pair_cost,
    )(projected, projected, mixed_all, packed_all, line_turned, stats_all)
    grads_low = jnp.concatenate([grad_query_low, grad_keys, grad_values], axis=1)
    grad_qkv = outer(normed1, grads_low).astype(jnp.bfloat16)
    qkv_sum = lax.psum_scatter(grad_qkv, "dp", scatter_dimension=0, tiled=True)
    grad_normed1 = dot_nt(grads_low, wqkv_all)
    grad_inputs, grad_gain_one = norm1_back(grad_normed1)
    grad_hidden = (grad_resid + grad_inputs)[None]
    onehot_sums = (
        jnp.arange(bucket_count, dtype=jnp.int32)[:, None] == seen_sums[None, :]
    ).astype(jnp.float32)
    grad_table = lax.dot_general(
        onehot_sums,
        diagonals.reshape(head_count, width),
        (((1,), (1,)), ((), ())),
        precision=HIGHEST,
    )
    small = jnp.concatenate(
        [grad_gain_one, grad_gain_two, grad_table.reshape(-1), grad_router.reshape(-1)]
    )
    small = lax.psum(small, ("dp", "expert"))
    matrix_sums = lax.psum(jnp.concatenate([qkv_sum, output_sum], axis=1), "expert").astype(
        jnp.float32
    )
    my_part = lax.axis_index("dp")
    part_count = model_width // w_query.shape[0]

    def mine(values):
        size = values.shape[0] // part_count
        return lax.dynamic_slice_in_dim(values, my_part * size, size, 0)

    table_end = 2 * model_width + bucket_count * head_count
    return (
        output[None],
        grad_hidden,
        mine(small[:model_width]),
        matrix_sums[:, :model_width],
        matrix_sums[:, model_width : 2 * model_width],
        matrix_sums[:, 2 * model_width : 3 * model_width],
        matrix_sums[:, 3 * model_width :],
        mine(small[2 * model_width : table_end].reshape(bucket_count, head_count)),
        mine(small[model_width : 2 * model_width]),
        mine(small[table_end:].reshape(model_width, experts)),
        first_sum.astype(jnp.float32)[None],
        second_sum.astype(jnp.float32).T[None],
    )


def solution(mesh):
    return jax.shard_map(
        on_device,
        mesh=mesh,
        in_specs=(
            P("dp", "expert", None),
            P("dp", "expert", None),
            P(),
            P("dp", None),
            P("dp", None),
            P("dp", None),
            P("dp", None),
            P(),
            P(),
            P("dp", None),
            P("expert", "dp", None),
            P("expert", None, "dp"),
            P("dp", "expert", None),
            P("dp", "expert", None),
            P(),
        ),
        out_specs=(
            P("dp", "expert", None),
            P("dp", "expert", None),
            P("dp"),
            P("dp", None),
            P("dp", None),
            P("dp", None),
            P("dp", None),
            P("dp", None),
            P("dp"),
            P("dp", None),
            P("expert", "dp", None),
            P("expert", None, "dp"),
        ),
        check_vma=False,
    )
```

time: 2360 us -> 746 us (0.32)
  local copies, waits for them, and re-layouts: 827 us -> 23.8 us
  starting transfers between devices: 501 us -> 4.32 us
  waiting for transfers between devices: 836 us -> 543 us
  Pallas kernels: 0 us -> 29.3 us
  matrix products: 77.8 us -> 49.4 us
    gather x8 -> x0, local copies, waits for them, and re-layouts: 713 us -> none  [the longest x6 709 us: block_scores(): bias_values = jnp.take(offset_bias, clipped, axis=1)]
    all_to_all x4 -> x1, starting transfers between devices: 500 us -> 3.69 us  [on_device(): lax.all_to_all(jnp.concatenate([expert_out, grad_rows], axis=1).reshape(e...]
    reduce_scatter x5 -> x3, waiting for transfers between devices: 541 us -> 157 us  [the longest x1 85.3 us: on_device(): lax.psum_scatter(grad_second, 'dp', scatter_dimension=0, tiled=True)]
    all_gather x8 -> x6, waiting for transfers between devices: 107 us -> 285 us  [the longest x1 83.4 us: on_device(): second_turned = lax.all_gather(w_out[0].T, 'dp', axis=0, tiled=True)]
    unnamed x19 -> x11, waiting for transfers between devices: 91.1 us -> 1.2 us
    unnamed x142 -> x77, local copies, waits for them, and re-layouts: 53.3 us -> 7.06 us
    psum x1, waiting for transfers between devices: 18.7 us -> 57.9 us  [on_device(): lax.psum(jnp.concatenate([qkv_sum, output_sum], axis=1), 'expert')]
    dot_general x28 -> x17, matrix products: 73 us -> 42.4 us  [the longest x4 16.2 us: outer(): lax.dot_general(left, right, (((0,), (0,)), ((), ())), preferred_element_...]
  transfers between devices with their start and end apart: 21 -> 12, of which waited for: 15 -> 12; matrix products, arithmetic and copies ran while one was open for 25% -> 8% of each run, Pallas kernels for 0% -> 4%
where the time goes in v1:
time: 746 us; the launch traced here: 745 us
  waiting for transfers between devices  543 us (73%)
  blocking collectives  62.3 us (8%)
  matrix products  49.4 us (7%)
  Pallas kernels  29.3 us (4%)
  local copies, waits for them, and re-layouts  23.8 us (3%)
  other arithmetic  17.7 us (2%)
  between operations  14.6 us (2%)
    reduce_scatter x1, waiting for transfers between devices, on_device(): lax.psum_scatter(grad_second, 'dp', scatter_dimension=0, tiled=True)  85.3 us
    all_gather x1, waiting for transfers between devices, on_device(): second_turned = lax.all_gather(w_out[0].T, 'dp', axis=0, tiled=True)  83.4 us
    all_gather x1, waiting for transfers between devices, on_device(): wqkv_all = lax.all_gather(wqkv, 'dp', axis=0, tiled=True)  72.7 us
    reduce_scatter x1, waiting for transfers between devices, on_device(): qkv_sum = lax.psum_scatter(grad_qkv, 'dp', scatter_dimension=0, tiled=True)  67.4 us
    all_gather x1, waiting for transfers between devices, on_device(): first_weight = lax.all_gather(w_in[0], 'dp', axis=0, tiled=True)  66.8 us
    psum x1, waiting for transfers between devices, on_device(): lax.psum(jnp.concatenate([qkv_sum, output_sum], axis=1), 'expert')  57.9 us
    psum x1, blocking collectives, on_device(): small = lax.psum(small, ('dp', 'expert'))  44.2 us
    all_gather x1, waiting for transfers between devices, on_device(): mixed_all = lax.all_gather(projected, 'expert', axis=0, tiled=True)  33.7 us
  transfers between devices with their start and end apart: 12, of which 12 were waited for; matrix products, arithmetic and copies ran while one was open for 8% of the time, Pallas kernels for 4%

profile of v1, /device:TPU:0, one launch (start us, length us, event | category | flops | bytes accessed | tf_op | source)
XLA Modules:
  0.0 744.9 jit_solution(2084462709102774252)
XLA Ops:
  7.3 2.2 pad_maximum_fusion.1
  10.2 72.7 %all-gather.8.cloned.1.call-done = bf16[768,2304]{1,0:T(8,128)(2,1)} async-done(((bf16[192,2304]{1,0:T(8,128)(2,1)}), bf16[768,2304]{1,0:T(8,128)(2,1)}) %all-gather.8.cloned.1.call-update) | async-done | bytes 3538960 | tf_op jit(solution)/shard_map/all_gather | solution.py:179
  82.9 3.5 convolution_convert_fusion.3.q_ref.k_ref.v_ref
  90.4 33.7 %all-gather.10.cloned.1.call-done.k_ref.v_ref.q_ref = bf16[1024,2304]{1,0:T(8,128)(2,1)} async-done(((bf16[128,2304]{1,0:T(8,128)(2,1)}), bf16[1024,2304]{1,0:T(8,128)(2,1)}) %all-gather.10.cloned.1.call-update) | async-done | bytes 4718608 | tf_op jit(solution)/shard_map/all_gather | solution.py:215
  124.1 9.5 %shard_map.238 = (bf16[128,768]{1,0:T(8,128)(2,1)}, f32[128,768]{1,0:T(8,128)}, f32[128,768]{1,0:T(8,128)}) custom-call(bf16[128,2304]{1,0:T(8,128)(2,1)} %convolution_convert_fusion.3.q_ref.k_ref.v_ref, bf16[1024,2304]{1,0:T(8,128)(2,1)} %all-gather.10.cloned.1.call-done.k_ref.v_ref.q_ref, ...), custom_call_target="tpu_custom_call" | custom-call | flops 603979776 | bytes 6039797 | tf_op jit(solution)/shard_map/pallas_call | solution.py:225
  133.6 26.6 %all-gather.12.cloned.1.call-done = bf16[768,896]{1,0:T(8,128)(2,1)} async-done(((bf16[192,896]{1,0:T(8,128)(2,1)}), bf16[768,896]{1,0:T(8,128)(2,1)}) %all-gather.12.cloned.1.call-update) | async-done | bytes 1376272 | tf_op jit(solution)/shard_map/all_gather | solution.py:180
  160.1 1.8 multiply_reduce_fusion.4
  162.0 1.5 fusion.90
  164.9 18.1 %all_to_all.10 = bf16[8,36,1536]{2,1,0:T(8,128)(2,1)S(1)} all-to-all(bf16[8,36,1536]{2,1,0:T(8,128)(2,1)S(1)} %reshape.261), channel_id=1, replica_groups=mesh['expert'=8,'dp'=4] {'expert'}, dimensions={0} | all-to-all | bytes 1769472 | tf_op jit(solution)/shard_map/all_to_all | solution.py:282
  183.2 66.8 %all-gather.18.cloned.1.call-done = bf16[1,768,3072]{2,1,0:T(8,128)(2,1)} async-done(((bf16[1,192,3072]{2,1,0:T(8,128)(2,1)}), bf16[1,768,3072]{2,1,0:T(8,128)(2,1)}) %all-gather.18.cloned.1.call-update) | async-done | bytes 4718608 | tf_op jit(solution)/shard_map/all_gather | solution.py:181
  249.9 5.9 multiply_convert_fusion
  255.9 83.4 %all-gather.14.cloned.1.call-done = bf16[768,3072]{1,0:T(8,128)(2,1)} async-done(((bf16[192,3072]{1,0:T(8,128)(2,1)}), bf16[768,3072]{1,0:T(8,128)(2,1)}) %all-gather.14.cloned.1.call-update) | async-done | bytes 4718608 | tf_op jit(solution)/shard_map/all_gather | solution.py:182
  339.3 6.0 fusion.4
  345.3 1.6 fusion.11
  346.9 1.3 copy-done.33
  348.8 1.6 convolution_convert_fusion.6
  350.5 1.2 reshape.263
  351.6 3.7 all-to-all-start.1
  355.9 14.2 %all-to-all-done.1 = bf16[8,36,1536]{2,1,0:T(8,128)(2,1)S(1)} async-done(((bf16[8,36,1536]{2,1,0:T(8,128)(2,1)}), bf16[8,36,1536]{2,1,0:T(8,128)(2,1)S(1)}, u32[]{:S(2)}, u32[]{:S(2)}) %all-to-all-start.1) | async-done | bytes 884768 | tf_op jit(solution)/shard_map/all_to_all | solution.py:295
  371.5 1.1 multiply_reduce_fusion.2
  375.5 5.8 convolution_convert_fusion.1
  382.3 1.5 convolution_convert_fusion.5
  384.9 11.9 %shard_map.239 = (bf16[128,768]{1,0:T(8,128)(2,1)}, f32[6,2,1152]{2,1,0:T(2,128)}) custom-call(bf16[128,2304]{1,0:T(8,128)(2,1)} %convolution_convert_fusion.3.q_ref.k_ref.v_ref, bf16[1024,2304]{1,0:T(8,128)(2,1)} %all-gather.10.cloned.1.call-done.k_ref.v_ref.q_ref, bf16[1024,2304]{1,0:T(8,128)(2,1)} %all-gather.10.cloned.1.call-done.k_ref.v_ref.q_ref, ...), custom_call_target="tpu_custom_call" | custom-call | flops 1006632960 | bytes 10066329 | tf_op jit(solution)/shard_map/pallas_call | solution.py:334
  396.7 0.9 constant_dynamic-update-slice_fusion.2
  397.6 1.4 all-gather.16.cloned.1.call-done.grad_ref
  399.0 1.0 slice_convert_fusion
  401.3 8.0 %shard_map.240 = (bf16[128,768]{1,0:T(8,128)(2,1)}, bf16[128,768]{1,0:T(8,128)(2,1)}) custom-call(bf16[128,2304]{1,0:T(8,128)(2,1)} %convolution_convert_fusion.3.q_ref.k_ref.v_ref, bf16[128,2304]{1,0:T(8,128)(2,1)} %convolution_convert_fusion.3.q_ref.k_ref.v_ref, bf16[1024,2304]{1,0:T(8,128)(2,1)} %all-gather.10.cloned.1.call-done.k_ref.v_ref.q_ref, ...), custom_call_target="tpu_custom_call" | custom-call | flops 805306368 | bytes 8053063 | tf_op jit(solution)/shard_map/pallas_call | solution.py:347
  409.3 0.9 constant_dynamic-update-slice_fusion.1
  410.2 0.9 constant_dynamic-update-slice_fusion
  411.2 3.0 convolution_convert_fusion.2
  414.3 5.8 convolution_convert_fusion
  420.1 1.5 dynamic_slice.23
  421.7 2.6 fusion.42
  424.3 1.8 reshape.273
  426.1 1.5 reshape.271
  427.6 1.7 fusion.58
  430.2 3.7 fusion.30
  433.9 44.2 %psum.14 = f32[8064]{0:T(1024)S(1)} all-reduce(f32[8064]{0:T(1024)S(1)} %pad_maximum_fusion.3), channel_id=1, replica_groups=mesh['expert'=8,'dp'=4] {'dp','expert'}, use_global_device_ids=true, to_apply=%region_19.20 | all-reduce | flops 8064 | bytes 64512 | tf_op jit(solution)/shard_map/psum | solution.py:380
  481.7 2.1 fusion.33
  483.8 3.9 reduce-scatter.9.cloned.1.call-done
  487.7 2.9 bitcast_convert_fusion
  490.6 29.1 %reduce-scatter.7.cloned.1.call-done = bf16[192,768]{1,0:T(8,128)(2,1)} async-done(((bf16[768,768]{1,0:T(8,128)(2,1)}), bf16[192,768]{1,0:T(8,128)(2,1)}) %reduce-scatter.7.cloned.1.call-update) | async-done | bytes 294928 | tf_op jit(solution)/shard_map/reduce_scatter | solution.py:343
  519.7 67.4 %reduce-scatter.5.cloned.1.call-done = bf16[192,2304]{1,0:T(8,128)(2,1)} async-done(((bf16[768,2304]{1,0:T(8,128)(2,1)}), bf16[192,2304]{1,0:T(8,128)(2,1)}) %reduce-scatter.5.cloned.1.call-update) | async-done | bytes 884752 | tf_op jit(solution)/shard_map/reduce_scatter | solution.py:364
  587.1 2.4 pad_maximum_fusion
  589.5 85.3 %reduce-scatter.11.cloned.1.call-done = bf16[192,3072]{1,0:T(8,128)(2,1)} async-done(((bf16[768,3072]{1,0:T(8,128)(2,1)}), bf16[192,3072]{1,0:T(8,128)(2,1)}) %reduce-scatter.11.cloned.1.call-update) | async-done | bytes 1179664 | tf_op jit(solution)/shard_map/reduce_scatter | solution.py:313
  674.8 2.9 convert_bitcast_fusion
  677.7 57.9 %all-reduce.5.cloned.1.call-done = bf16[192,3072]{1,0:T(8,128)(2,1)} async-done(((bf16[192,3072]{1,0:T(8,128)(2,1)}), bf16[192,3072]{1,0:T(8,128)(2,1)}) %all-reduce.5.cloned.1.call-update) | async-done | bytes 1179664 | tf_op jit(solution)/shard_map/psum | solution.py:381
  735.7 2.7 fusion.87
  (181 shorter events, 19.3 us)
Async XLA Ops:
  7.2 82.2 %copy-start = (f32[32,12]{0,1:T(8,128)S(1)}, f32[32,12]{0,1:T(8,128)}, u32[]{:S(2)}) copy-start(f32[32,12]{0,1:T(8,128)} %param.22) | copy-start | bytes 4612
  7.2 2.3 copy-start.4
  7.2 75.7 %copy-start.18 = (f32[768]{0:T(1024)S(1)}, f32[768]{0:T(1024)}, u32[]{:S(2)}) copy-start(f32[768]{0:T(1024)} %param.17) | copy-start | bytes 9220
  7.2 75.7 %all-gather.8.cloned.1.call-start = ((), (), s32[]{:S(2)}) async-start(), calls=%async_computation.6 | async-start | bytes 4423680 | tf_op jit(solution)/shard_map/all_gather | solution.py:179
  9.4 114.7 %all-gather.10.cloned.1.call-start = ((), (), s32[]{:S(2)}) async-start(), calls=%async_computation.7 | async-start | bytes 5308416 | tf_op jit(solution)/shard_map/all_gather | solution.py:215
  9.6 0.6 copy-start.31
  10.2 401.0 %copy-start.28 = (f32[128]{0:T(128)}, f32[128]{0:T(128)S(1)}, u32[]{:S(2)}) copy-start(f32[128]{0:T(128)S(1)} %fusion.82) | copy-start | bytes 1540
  10.2 76.3 %copy-start.29 = (bf16[192,8]{0,1:T(8,128)(2,1)S(1)}, bf16[192,8]{0,1:T(8,128)(2,1)}, u32[]{:S(2)}) copy-start(bf16[192,8]{0,1:T(8,128)(2,1)} %param.24) | copy-start | bytes 9220
  10.2 76.5 %copy-start.13 = (bf16[192,768]{1,0:T(8,128)(2,1)S(1)}, bf16[192,768]{1,0:T(8,128)(2,1)}, u32[]{:S(2)}) copy-start(bf16[192,768]{1,0:T(8,128)(2,1)} %param.21) | copy-start | bytes 884740
  86.4 2.2 copy-start.24
  86.4 3.9 copy-start.21
  86.4 3.9 copy-start.12
  86.5 73.7 %all-gather.12.cloned.1.call-start = ((), (), s32[]{:S(2)}) async-start(), calls=%async_computation.8 | async-start | bytes 1720320 | tf_op jit(solution)/shard_map/all_gather | solution.py:180
  87.5 162.5 %all-gather.18.cloned.1.call-start = ((), (), s32[]{:S(2)}) async-start(), calls=%async_computation.16 | async-start | bytes 5898240 | tf_op jit(solution)/shard_map/all_gather | solution.py:181
  88.0 251.2 %all-gather.14.cloned.1.call-start = ((), (), s32[]{:S(2)}) async-start(), calls=%async_computation.9 | async-start | bytes 5898240 | tf_op jit(solution)/shard_map/all_gather | solution.py:182
  88.8 0.6 copy-start.20
  90.4 71.6 %copy-start.15 = (f32[768]{0:T(1024)S(1)}, f32[768]{0:T(1024)}, u32[]{:S(2)}) copy-start(f32[768]{0:T(1024)} %param.23) | copy-start | bytes 9220
  133.6 29.9 %copy-start.26 = (s32[1,128,2]{1,2,0:T(2,128)S(1)}, s32[1,128,2]{1,2,0:T(2,128)}, u32[]{:S(2)}) copy-start(s32[1,128,2]{1,2,0:T(2,128)} %param.27) | copy-start | bytes 3076
  161.9 210.7 %copy-start.2 = (f32[128,768]{1,0:T(8,128)}, f32[128,768]{1,0:T(8,128)S(1)}, u32[]{:S(2)}) copy-start(f32[128,768]{1,0:T(8,128)S(1)} %get-tuple-element.93) | copy-start | bytes 1179652
  162.0 210.6 %copy-start.25 = (f32[128]{0:T(128)}, f32[128]{0:T(128)S(1)}, u32[]{:S(2)}) copy-start(f32[128]{0:T(128)S(1)} %fusion.83) | copy-start | bytes 1540
  163.5 207.7 %copy-start.22 = (f32[128]{0:T(128)}, f32[128]{0:T(128)S(1)}, u32[]{:S(2)}) copy-start(f32[128]{0:T(128)S(1)} %get-tuple-element.94) | copy-start | bytes 1540
  163.5 207.7 %copy-start.27 = (f32[128]{0:T(128)}, f32[128]{0:T(128)S(1)}, u32[]{:S(2)}) copy-start(f32[128]{0:T(128)S(1)} %fusion.81) | copy-start | bytes 1540
  183.1 156.1 %copy-start.10 = (bf16[288,1536]{1,0:T(8,128)(2,1)}, bf16[288,1536]{1,0:T(8,128)(2,1)S(1)}, u32[]{:S(2)}) copy-start(bf16[288,1536]{1,0:T(8,128)(2,1)S(1)} %reshape.262) | copy-start | bytes 2654212
  339.2 6.0 copy-start.32
  345.2 1.6 copy-start.35
  345.2 3.0 copy-start.33
  345.2 3.5 copy-start.34
  350.4 5.1 copy-start.9
  351.6 18.4 %all-to-all-start.1 = ((bf16[8,36,1536]{2,1,0:T(8,128)(2,1)}), bf16[8,36,1536]{2,1,0:T(8,128)(2,1)S(1)}, u32[]{:S(2)}, u32[]{:S(2)}) async-start(bf16[8,36,1536]{2,1,0:T(8,128)(2,1)} %reshape.263), calls=%async_computation.1 | async-start | bytes 1966080 | tf_op jit(solution)/shard_map/all_to_all | solution.py:295
  355.3 43.7 %all-gather.16.cloned.1.call-start = ((), (), s32[]{:S(2)}) async-start(), calls=%async_computation.10 | async-start | bytes 2064384 | tf_op jit(solution)/shard_map/all_gather | solution.py:333
  370.2 1.3 copy-start.6
  370.8 2.6 copy-start.8
  371.1 2.3 copy-start.17
  371.5 2.4 copy-start.30
  373.4 8.0 %copy-start.3 = (f32[128,768]{1,0:T(8,128)}, f32[128,768]{1,0:T(8,128)S(1)}, u32[]{:S(2)}) copy-start(f32[128,768]{1,0:T(8,128)S(1)} %get-tuple-element.74) | copy-start | bytes 1179652
  373.4 2.1 copy-start.11
  373.9 7.4 copy-start.7
  375.4 112.2 %reduce-scatter.9.cloned.1.call-start = ((), (), s32[]{:S(2)}) async-start(), calls=%async_computation.14 | async-start | bytes 5898240 | tf_op jit(solution)/shard_map/reduce_scatter | solution.py:312
  381.3 0.9 copy-start.14
  381.4 138.3 %reduce-scatter.7.cloned.1.call-start = ((), (), s32[]{:S(2)}) async-start(), calls=%async_computation.12 | async-start | bytes 1474560 | tf_op jit(solution)/shard_map/reduce_scatter | solution.py:343
  383.8 203.3 %reduce-scatter.5.cloned.1.call-start = ((), (), s32[]{:S(2)}) async-start(), calls=%async_computation.11 | async-start | bytes 4423680 | tf_op jit(solution)/shard_map/reduce_scatter | solution.py:364
  411.2 3.0 copy-start.5
  414.2 260.6 %reduce-scatter.11.cloned.1.call-start = ((), (), s32[]{:S(2)}) async-start(), calls=%async_computation.15 | async-start | bytes 5898240 | tf_op jit(solution)/shard_map/reduce_scatter | solution.py:313
  420.1 10.1 %copy-start.1 = (bf16[768,2304]{1,0:T(8,128)(2,1)S(1)}, bf16[768,2304]{1,0:T(8,128)(2,1)}, u32[]{:S(2)}) copy-start(bf16[768,2304]{1,0:T(8,128)(2,1)} %all-gather.8.cloned.1.call-done) | copy-start | bytes 10616836
  420.1 315.6 %all-reduce.5.cloned.1.call-start = ((), (), s32[]{:S(2)}) async-start(), calls=%async_computation.13 | async-start | bytes 2359296 | tf_op jit(solution)/shard_map/psum | solution.py:381
  430.1 3.8 copy-start.16
  430.1 3.8 copy-start.23
  430.1 51.6 %copy-start.19 = (f32[768]{0:T(1024)S(1)}, f32[768]{0:T(1024)}, u32[]{:S(2)}) copy-start(f32[768]{0:T(1024)} %param.17) | copy-start | bytes 9220
Sparse Core Ops, SparseCore 0:
  10.2 72.6 all-gather.7
  86.6 37.4 all-gather.9
  126.3 33.8 all-gather.11
  161.6 88.3 all-gather.17
  251.3 87.8 all-gather.13
  375.6 23.4 all-gather.15
  401.3 86.2 reduce-scatter.8
  490.0 29.6 reduce-scatter.6
  522.0 65.0 reduce-scatter.4
  589.2 85.5 reduce-scatter.10
  678.0 57.6 all-reduce.4

commit v2 on v1

--- a/solution.py
+++ b/solution.py
@@ -133,6 +133,27 @@
         cost_estimate=pl.CostEstimate(flops=cost, bytes_accessed=cost // 100, transcendentals=0),
         compiler_params=pltpu.CompilerParams(vmem_limit_bytes=VMEM_BYTES),
     )
+
+
+def ring_step(values, count):
+    return lax.ppermute(values, "dp", [(part, (part + 1) % count) for part in range(count)])
+
+
+def ring_blocks(block, count):
+    blocks = [block]
+    for _ in range(count - 1):
+        blocks.append(ring_step(blocks[-1], count))
+    return blocks
+
+
+def ring_sum(term, count):
+    running = term(1).astype(jnp.bfloat16) if count > 1 else None
+    for place in range(2, count):
+        arrived = ring_step(running, count).astype(jnp.float32)
+        running = (arrived + term(place)).astype(jnp.bfloat16)
+    if count == 1:
+        return term(0)
+    return ring_step(running, count).astype(jnp.float32) + term(0)
 
 
 def split_three(values):
@@ -172,16 +193,47 @@
     query_start = my_index * tok_rows
     width = seq_len + tok_rows
 
-    wqkv = jnp.concatenate([w_query, w_key, w_value], axis=1)
-    wrest = jnp.concatenate(
-        [w_output, jnp.pad(w_router, ((0, 0), (0, LANES - experts)))], axis=1
-    )
-    wqkv_all = lax.all_gather(wqkv, "dp", axis=0, tiled=True)
-    wrest_all = lax.all_gather(wrest, "dp", axis=0, tiled=True)
-    first_weight = lax.all_gather(w_in[0], "dp", axis=0, tiled=True)
-    second_turned = lax.all_gather(w_out[0].T, "dp", axis=0, tiled=True)
-    output_all = wrest_all[:, :model_width]
-    router = wrest_all[:, model_width : model_width + experts].astype(jnp.float32)
+    part_rows = w_query.shape[0]
+    part_count = model_width // part_rows
+    my_part = lax.axis_index("dp")
+    lines = lax.axis_size("expert")
+    share = part_rows // lines
+    first_blocks = ring_blocks(w_in[0], part_count)
+    second_blocks = ring_blocks(w_out[0].T, part_count)
+    first_weight = jnp.concatenate(first_blocks, axis=0)
+    second_turned = jnp.concatenate(second_blocks, axis=0)
+
+    def my_share(matrix):
+        return lax.dynamic_slice_in_dim(matrix, my_index * share, share, 0)
+
+    mixer_share = jnp.concatenate(
+        [
+            my_share(w_query),
+            my_share(w_key),
+            my_share(w_value),
+            my_share(w_output),
+            jnp.pad(my_share(w_router), ((0, 0), (0, LANES - experts))),
+        ],
+        axis=1,
+    )
+    mixer_all = lax.all_gather(mixer_share, ("dp", "expert"), axis=0, tiled=True)
+    wqkv_all = mixer_all[:, : 3 * model_width]
+    output_all = mixer_all[:, 3 * model_width : 4 * model_width]
+    router = mixer_all[:, 4 * model_width : 4 * model_width + experts].astype(jnp.float32)
+
+    def turn(values):
+        blocks = [
+            values[:, part * part_rows : (part + 1) * part_rows]
+            for part in range(part_count - 1, -1, -1)
+        ]
+        doubled = jnp.concatenate(blocks + blocks, axis=1)
+        return lax.dynamic_slice_in_dim(
+            doubled, (part_count - 1 - my_part) * part_rows, model_width, 1
+        )
+
+    def by_line(values):
+        shaped = values.reshape(tok_rows, part_count, lines, share)
+        return jnp.transpose(shaped, (0, 2, 1, 3)).reshape(tok_rows, model_width)
 
     def filler(count):
         return jnp.full((count,), bucket_count, jnp.int32)
@@ -212,12 +264,13 @@
     normed1_f, norm1_back = jax.vjp(rms_norm, inputs, norm1_gain)
     normed1 = normed1_f.astype(jnp.bfloat16)
     projected = jnp.dot(normed1, wqkv_all, preferred_element_type=jnp.float32).astype(jnp.bfloat16)
-    mixed_all = lax.all_gather(projected, "expert", axis=0, tiled=True)
+    mixed_all = lax.all_gather(projected[:, model_width:], "expert", axis=0, tiled=True)
+    queries_all = lax.all_gather(projected[:, :model_width], "expert", axis=0, tiled=True)
     pair_cost = 2 * tok_rows * seq_len * model_width
     mixer_specs = [
         columns(tok_rows, 0),
+        columns(seq_len, 0),
         columns(seq_len, pairs),
-        columns(seq_len, 2 * pairs),
         planes(2, width),
     ]
     wide_shape = jax.ShapeDtypeStruct((tok_rows, model_width), jnp.float32)
@@ -245,7 +298,9 @@
     (normed2_f, gates), route_back = jax.vjp(route, resid, norm2_gain, router)
     normed2 = normed2_f.astype(jnp.bfloat16)
     grad_top = cotangent[0].astype(jnp.float32)
-    grad_made = (gates[:, :, None] * grad_top[:, None, :]).astype(jnp.bfloat16)
+    grad_turned = turn(cotangent[0]).astype(jnp.float32)
+    grad_made = (gates[:, :, None] * grad_turned[:, None, :]).astype(jnp.bfloat16)
+    normed_turned = turn(normed2)
     markers = chosen * kept[:, :, None]
     both = markers.reshape(tok_rows, 2 * experts).astype(jnp.bfloat16)
     row_number = jnp.arange(tok_rows, dtype=jnp.int32)
@@ -267,8 +322,8 @@
     ).astype(jnp.bfloat16)
     rows_out = jnp.concatenate(
         [
-            jnp.concatenate([normed2, grad_made[:, 0]], axis=1),
-            jnp.concatenate([normed2, grad_made[:, 1]], axis=1),
+            jnp.concatenate([normed_turned, grad_made[:, 0]], axis=1),
+            jnp.concatenate([normed_turned, grad_made[:, 1]], axis=1),
         ],
         axis=0,
     )
@@ -307,17 +362,20 @@
             left, right, (((0,), (0,)), ((), ())), preferred_element_type=jnp.float32
         )
 
-    grad_first = outer(arrived, grad_pre).astype(jnp.bfloat16)
-    grad_second = outer(grad_arrived, activated).astype(jnp.bfloat16)
-    first_sum = lax.psum_scatter(grad_first, "dp", scatter_dimension=0, tiled=True)
-    second_sum = lax.psum_scatter(grad_second, "dp", scatter_dimension=0, tiled=True)
-    back = jnp.dot(placing, returned, preferred_element_type=jnp.float32).reshape(
-        2, tok_rows, 2 * model_width
-    )
-    picked_rows = jnp.transpose(back[:, :, :model_width], (1, 0, 2))
+    def feature_block(values, place):
+        return values[:, place * part_rows : (place + 1) * part_rows]
+
+    first_sum = ring_sum(lambda place: outer(feature_block(arrived, place), grad_pre), part_count)
+    second_sum = ring_sum(
+        lambda place: outer(feature_block(grad_arrived, place), activated), part_count
+    )
+    back = jnp.dot(placing, returned, preferred_element_type=jnp.float32).astype(jnp.bfloat16)
+    made_back = turn(back[:, :model_width]).astype(jnp.float32)
+    rows_back = turn(back[:, model_width:]).astype(jnp.float32)
+    picked_rows = jnp.stack([made_back[:tok_rows], made_back[tok_rows:]], axis=1)
     output = (resid + jnp.sum(gates[:, :, None] * picked_rows, axis=1)).astype(jnp.bfloat16)
     grad_gates = jnp.sum(picked_rows * grad_top[:, None, :], axis=-1)
-    grad_normed2 = back[0, :, model_width:] + back[1, :, model_width:]
+    grad_normed2 = rows_back[:tok_rows] + rows_back[tok_rows:]
     grad_resid_norm, grad_gain_two, grad_router = route_back((grad_normed2, grad_gates))
     grad_resid = grad_top + grad_resid_norm
     grad_branch = grad_resid.astype(jnp.bfloat16)
@@ -339,8 +397,7 @@
         [low_shape, jax.ShapeDtypeStruct((pairs, 2, width), jnp.float32)],
         5 * pair_cost,
     )(projected, mixed_all, mixed_all, line, grad_attended, exact_out, log_wide)
-    grad_output = outer(attended, grad_branch).astype(jnp.bfloat16)
-    output_sum = lax.psum_scatter(grad_output, "dp", scatter_dimension=0, tiled=True)
+    grad_output = outer(by_line(attended), grad_branch).astype(jnp.bfloat16)
     stats_all = packed_all[:, model_width : model_width + 6 * head_count].astype(jnp.float32)
     stats_all = jnp.sum(stats_all.reshape(seq_len, 2, 3, pairs, 2), axis=2)
     stats_all = jnp.transpose(stats_all, (2, 1, 3, 0)).reshape(pairs, 4, seq_len)
@@ -358,10 +415,13 @@
         [columns(tok_rows, 0)] * 2,
         [low_shape, low_shape],
         4 * pair_cost,
-    )(projected, projected, mixed_all, packed_all, line_turned, stats_all)
+    )(projected, projected, queries_all, packed_all, line_turned, stats_all)
     grads_low = jnp.concatenate([grad_query_low, grad_keys, grad_values], axis=1)
-    grad_qkv = outer(normed1, grads_low).astype(jnp.bfloat16)
-    qkv_sum = lax.psum_scatter(grad_qkv, "dp", scatter_dimension=0, tiled=True)
+    grad_qkv = outer(by_line(normed1), grads_low).astype(jnp.bfloat16)
+    grad_mixer = jnp.concatenate([grad_qkv, grad_output], axis=1)
+    line_sum = lax.psum_scatter(grad_mixer, "expert", scatter_dimension=0, tiled=True)
+    part_sum = lax.psum_scatter(line_sum, "dp", scatter_dimension=0, tiled=True)
+    matrix_sums = lax.all_gather(part_sum, "expert", axis=0, tiled=True).astype(jnp.float32)
     grad_normed1 = dot_nt(grads_low, wqkv_all)
     grad_inputs, grad_gain_one = norm1_back(grad_normed1)
     grad_hidden = (grad_resid + grad_inputs)[None]
@@ -378,11 +438,6 @@
         [grad_gain_one, grad_gain_two, grad_table.reshape(-1), grad_router.reshape(-1)]
     )
     small = lax.psum(small, ("dp", "expert"))
-    matrix_sums = lax.psum(jnp.concatenate([qkv_sum, output_sum], axis=1), "expert").astype(
-        jnp.float32
-    )
-    my_part = lax.axis_index("dp")
-    part_count = model_width // w_query.shape[0]
 
     def mine(values):
         size = values.shape[0] // part_count

time: 746 us -> 599 us (0.80)
  waiting for transfers between devices: 543 us -> 347 us
  local copies, waits for them, and re-layouts: 23.8 us -> 63.7 us
  blocking collectives: 62.3 us -> 37.7 us
  other arithmetic: 17.7 us -> 36.7 us
  starting transfers between devices: 4.32 us -> 14.5 us
    ppermute x0 -> x12, waiting for transfers between devices: none -> 257 us  [ring_step(): lax.ppermute(values, 'dp', [(part, (part + 1) % count) for part in range(...]
    all_gather x5 -> x4, waiting for transfers between devices: 283 us -> 75.6 us  [the longest x1 65.5 us: on_device(): lax.all_gather(mixer_share, ('dp', 'expert'), axis=0, tiled=True)]
    reduce_scatter x4 -> x2, waiting for transfers between devices: 186 us -> 0.01 us  [the longest x1 0.01 us: on_device(): lax.psum_scatter(grad_mixer, 'expert', scatter_dimension=0, tiled=True)]
    psum x1 -> x0, waiting for transfers between devices: 57.9 us -> none  [on_device(): lax.psum(jnp.concatenate([qkv_sum, output_sum], axis=1), 'expert')]
    all_to_all x1 -> x0, blocking collectives: 18.1 us -> none  [on_device(): lax.all_to_all(outgoing, 'expert', split_axis=0, concat_axis=0, tiled=True)]
    all_to_all x1, waiting for transfers between devices: 14.2 us -> 4.32 us  [on_device(): lax.all_to_all(jnp.concatenate([expert_out, grad_rows], axis=1).reshape(e...]
    all_to_all x0 -> x1, waiting for transfers between devices: none -> 9.47 us  [on_device(): lax.all_to_all(outgoing, 'expert', split_axis=0, concat_axis=0, tiled=True)]
    dot_general x4 -> x10, matrix products: 16.2 us -> 19.7 us  [outer(): lax.dot_general(left, right, (((0,), (0,)), ((), ())), preferred_element_...]
  transfers between devices with their start and end apart: 12 -> 21, of which waited for: 12 -> 16; matrix products, arithmetic and copies ran while one was open for 8% -> 15% of each run, Pallas kernels for 4% -> 4%
where the time goes in v2:
time: 599 us; the launch traced here: 597 us
  waiting for transfers between devices  347 us (58%)
  local copies, waits for them, and re-layouts  63.7 us (11%)
  matrix products  53 us (9%)
  blocking collectives  37.7 us (6%)
  other arithmetic  36.7 us (6%)
  Pallas kernels  29.2 us (5%)
  between operations  15.3 us (3%)
  starting transfers between devices  14.5 us (2%)
    ppermute x12, waiting for transfers between devices, ring_step(): lax.ppermute(values, 'dp', [(part, (part + 1) % count) for part in range(...  257 us
    all_gather x1, waiting for transfers between devices, on_device(): lax.all_gather(mixer_share, ('dp', 'expert'), axis=0, tiled=True)  65.5 us
    psum x1, blocking collectives, on_device(): small = lax.psum(small, ('dp', 'expert'))  37.7 us
    dot_general x10, matrix products, outer(): lax.dot_general(left, right, (((0,), (0,)), ((), ())), preferred_element_...  19.7 us
    dot_general x4, matrix products, dot_nt(): lax.dot_general(left, right, (((1,), (1,)), ((), ())), preferred_element_...  12.7 us
    unnamed x141, local copies, waits for them, and re-layouts  12.4 us
  transfers between devices with their start and end apart: 21, of which 16 were waited for; matrix products, arithmetic and copies ran while one was open for 15% of the time, Pallas kernels for 4%

profile of v2, /device:TPU:0, one launch (start us, length us, event | category | flops | bytes accessed | tf_op | source)
XLA Modules:
  0.0 596.8 jit_solution(7405249569579611406)
XLA Ops:
  13.6 65.5 %all-gather.6.cloned.1.call-done = bf16[768,3200]{1,0:T(8,128)(2,1)} async-done(((bf16[24,3200]{1,0:T(8,128)(2,1)}), bf16[768,3200]{1,0:T(8,128)(2,1)}) %all-gather.6.cloned.1.call-update) | async-done | bytes 4915216 | tf_op jit(solution)/shard_map/all_gather | solution.py:219
  79.1 2.8 convolution_convert_fusion.3.q_ref.k_ref.v_ref
  82.8 1.9 collective-permute-start
  85.5 28.0 %collective-permute-done = bf16[192,3072]{1,0:T(8,128)(2,1)} collective-permute-done((bf16[192,3072]{1,0:T(8,128)(2,1)S(1)}, bf16[192,3072]{1,0:T(8,128)(2,1)}, u32[]{:S(2)}, u32[]{:S(2)}) %collective-permute-start) | collective-permute-done | bytes 1179680 | tf_op jit(solution)/shard_map/ppermute | solution.py:139
  115.8 23.0 %collective-permute-done.3 = bf16[192,3072]{1,0:T(8,128)(2,1)} collective-permute-done((bf16[192,3072]{1,0:T(8,128)(2,1)}, bf16[192,3072]{1,0:T(8,128)(2,1)}, u32[]{:S(2)}, u32[]{:S(2)}) %collective-permute-start.3) | collective-permute-done | bytes 1179680 | tf_op jit(solution)/shard_map/ppermute | solution.py:139
  138.9 25.2 %collective-permute-done.1 = bf16[192,3072]{1,0:T(8,128)(2,1)} collective-permute-done((bf16[192,3072]{1,0:T(8,128)(2,1)}, bf16[192,3072]{1,0:T(8,128)(2,1)}, u32[]{:S(2)}, u32[]{:S(2)}) %collective-permute-start.1) | collective-permute-done | bytes 1179680 | tf_op jit(solution)/shard_map/ppermute | solution.py:139
  164.2 9.4 %shard_map.238 = (bf16[128,768]{1,0:T(8,128)(2,1)}, f32[128,768]{1,0:T(8,128)}, f32[128,768]{1,0:T(8,128)}) custom-call(bf16[128,2304]{1,0:T(8,128)(2,1)} %copy-done.1, bf16[1024,1536]{1,0:T(8,128)(2,1)} %all-gather.8.cloned.1.call-done.k_ref.v_ref, bf16[1024,1536]{1,0:T(8,128)(2,1)} %all-gather.8.cloned.1.call-done.k_ref.v_ref, f32[6,2,1152]{2,1,0:T(2,128)} %reshape.256.line_ref), custom_call_target="tpu_custom_call" | custom-call | flops 603979776 | bytes 6039797 | tf_op jit(solution)/shard_map/pallas_call | solution.py:278
  180.7 3.6 all-to-all-start
  184.3 5.1 collective-permute-done.4
  189.4 9.5 %all-to-all-done = bf16[8,36,1536]{2,1,0:T(8,128)(2,1)S(1)} async-done(((bf16[8,36,1536]{2,1,0:T(8,128)(2,1)}), bf16[8,36,1536]{2,1,0:T(8,128)(2,1)S(1)}, u32[]{:S(2)}, u32[]{:S(2)}) %all-to-all-start) | async-done | bytes 884768 | tf_op jit(solution)/shard_map/all_to_all | solution.py:337
  199.1 15.5 %collective-permute-done.2 = bf16[192,3072]{1,0:T(8,128)(2,1)} collective-permute-done((bf16[192,3072]{1,0:T(8,128)(2,1)}, bf16[192,3072]{1,0:T(8,128)(2,1)}, u32[]{:S(2)}, u32[]{:S(2)}) %collective-permute-start.2) | collective-permute-done | bytes 1179680 | tf_op jit(solution)/shard_map/ppermute | solution.py:139
  214.6 4.3 multiply_convert_fusion
  219.0 20.3 %collective-permute-done.5 = bf16[192,3072]{1,0:T(8,128)(2,1)} collective-permute-done((bf16[192,3072]{1,0:T(8,128)(2,1)}, bf16[192,3072]{1,0:T(8,128)(2,1)}, u32[]{:S(2)}, u32[]{:S(2)}) %collective-permute-start.5) | collective-permute-done | bytes 1179680 | tf_op jit(solution)/shard_map/ppermute | solution.py:139
  239.3 3.8 fusion
  243.1 3.3 convolution_convert_fusion.7
  246.4 3.3 convolution_convert_fusion.8
  250.7 2.2 reshape.259
  252.8 4.2 all-to-all-start.1
  259.0 1.9 copy.59
  267.5 4.3 all-to-all-done.1
  271.8 2.2 reshape.260
  276.9 2.3 concatenate.89
  279.2 2.3 concatenate.88
  283.9 2.1 multiply_reduce_fusion.2
  287.5 2.6 convert_multiply_fusion
  290.1 1.9 copy.61
  319.2 11.9 %shard_map.239 = (bf16[128,768]{1,0:T(8,128)(2,1)}, f32[6,2,1152]{2,1,0:T(2,128)}) custom-call(bf16[128,2304]{1,0:T(8,128)(2,1)} %copy-done.1, bf16[1024,1536]{1,0:T(8,128)(2,1)} %all-gather.8.cloned.1.call-done.k_ref.v_ref, bf16[1024,1536]{1,0:T(8,128)(2,1)} %all-gather.8.cloned.1.call-done.k_ref.v_ref, f32[6,2,1152]{2,1,0:T(2,128)} %reshape.256.line_ref, ...), custom_call_target="tpu_custom_call" | custom-call | flops 1006632960 | bytes 10066329 | tf_op jit(solution)/shard_map/pallas_call | solution.py:392
  335.9 2.0 copy.65
  344.6 10.1 %all-gather.10.cloned.1.call-done.q_ref = bf16[1024,768]{1,0:T(8,128)(2,1)} async-done(((bf16[128,768]{1,0:T(8,128)(2,1)}), bf16[1024,768]{1,0:T(8,128)(2,1)}) %all-gather.10.cloned.1.call-update) | async-done | bytes 1572880 | tf_op jit(solution)/shard_map/all_gather | solution.py:268
  354.8 7.9 %shard_map.240 = (bf16[128,768]{1,0:T(8,128)(2,1)}, bf16[128,768]{1,0:T(8,128)(2,1)}) custom-call(bf16[128,2304]{1,0:T(8,128)(2,1)} %copy-done.1, bf16[128,2304]{1,0:T(8,128)(2,1)} %copy-done.1, bf16[1024,768]{1,0:T(8,128)(2,1)} %all-gather.10.cloned.1.call-done.q_ref, bf16[1024,896]{1,0:T(8,128)(2,1)} %all-gather.12.cloned.1.call-done.grad_ref, ...), custom_call_target="tpu_custom_call" | custom-call | flops 805306368 | bytes 8053063 | tf_op jit(solution)/shard_map/pallas_call | solution.py:404
  366.6 2.8 pad_maximum_fusion.2
  369.5 2.8 convolution_convert_fusion.2
  373.8 2.9 convolution_convert_fusion.1
  379.5 3.2 fusion.60
  382.8 20.4 %collective-permute-done.6 = bf16[192,3072]{1,0:T(8,128)(2,1)} collective-permute-done((bf16[192,3072]{1,0:T(8,128)(2,1)}, bf16[192,3072]{1,0:T(8,128)(2,1)}, u32[]{:S(2)}, u32[]{:S(2)}) %collective-permute-start.6) | collective-permute-done | bytes 1179680 | tf_op jit(solution)/shard_map/ppermute | solution.py:139
  403.2 2.1 add_convert_fusion.3
  406.3 22.2 %collective-permute-done.9 = bf16[192,3072]{1,0:T(8,128)(2,1)} collective-permute-done((bf16[192,3072]{1,0:T(8,128)(2,1)}, bf16[192,3072]{1,0:T(8,128)(2,1)}, u32[]{:S(2)}, u32[]{:S(2)}) %collective-permute-start.9) | collective-permute-done | bytes 1179680 | tf_op jit(solution)/shard_map/ppermute | solution.py:139
  428.5 2.1 add_convert_fusion.1
  430.7 2.2 fusion.51
  433.8 19.9 %collective-permute-done.7 = bf16[192,3072]{1,0:T(8,128)(2,1)S(1)} collective-permute-done((bf16[192,3072]{1,0:T(8,128)(2,1)S(1)}, bf16[192,3072]{1,0:T(8,128)(2,1)S(1)}, u32[]{:S(2)}, u32[]{:S(2)}) %collective-permute-start.7) | collective-permute-done | bytes 1179680 | tf_op jit(solution)/shard_map/ppermute | solution.py:139
  455.1 23.9 %collective-permute-done.10 = bf16[192,3072]{1,0:T(8,128)(2,1)S(1)} collective-permute-done((bf16[192,3072]{1,0:T(8,128)(2,1)S(1)}, bf16[192,3072]{1,0:T(8,128)(2,1)S(1)}, u32[]{:S(2)}, u32[]{:S(2)}) %collective-permute-start.10) | collective-permute-done | bytes 1179680 | tf_op jit(solution)/shard_map/ppermute | solution.py:139
  481.9 32.0 %collective-permute-done.8 = bf16[192,3072]{1,0:T(8,128)(2,1)} collective-permute-done((bf16[192,3072]{1,0:T(8,128)(2,1)}, bf16[192,3072]{1,0:T(8,128)(2,1)}, u32[]{:S(2)}, u32[]{:S(2)}) %collective-permute-start.8) | collective-permute-done | bytes 1179680 | tf_op jit(solution)/shard_map/ppermute | solution.py:139
  513.9 3.0 add_bitcast_fusion.1
  516.9 21.6 %collective-permute-done.11 = bf16[192,3072]{1,0:T(8,128)(2,1)} collective-permute-done((bf16[192,3072]{1,0:T(8,128)(2,1)}, bf16[192,3072]{1,0:T(8,128)(2,1)}, u32[]{:S(2)}, u32[]{:S(2)}) %collective-permute-start.11) | collective-permute-done | bytes 1179680 | tf_op jit(solution)/shard_map/ppermute | solution.py:139
  538.5 3.7 add_bitcast_fusion
  542.2 3.4 fusion.31
  545.7 37.7 %psum.7 = f32[8064]{0:T(1024)S(1)} all-reduce(f32[8064]{0:T(1024)S(1)} %pad_maximum_fusion.9), channel_id=1, replica_groups=mesh['expert'=8,'dp'=4] {'dp','expert'}, use_global_device_ids=true, to_apply=%region_19.20 | all-reduce | flops 8064 | bytes 64512 | tf_op jit(solution)/shard_map/psum | solution.py:440
  587.3 2.7 fusion.99
  (286 shorter events, 90.4 us)
Async XLA Ops:
  7.2 107.2 %copy-start = (f32[32,12]{0,1:T(8,128)S(1)}, f32[32,12]{0,1:T(8,128)}, u32[]{:S(2)}) copy-start(f32[32,12]{0,1:T(8,128)} %param.22) | copy-start | bytes 4612
  7.2 71.9 %all-gather.6.cloned.1.call-start = ((), (), s32[]{:S(2)}) async-start(), calls=%async_computation.4 | async-start | bytes 5068800 | tf_op jit(solution)/shard_map/all_gather | solution.py:219
  11.9 152.3 %all-gather.8.cloned.1.call-start = ((), (), s32[]{:S(2)}) async-start(), calls=%async_computation.5 | async-start | bytes 3538944 | tf_op jit(solution)/shard_map/all_gather | solution.py:267
  13.6 68.4 %copy-start.55 = (f32[128]{0:T(128)}, f32[128]{0:T(128)S(1)}, u32[]{:S(2)}) copy-start(f32[128]{0:T(128)S(1)} %fusion.91) | copy-start | bytes 1540
  13.6 69.2 %copy-start.61 = (bf16[1,192,3072]{2,1,0:T(8,128)(2,1)S(1)}, bf16[1,192,3072]{2,1,0:T(8,128)(2,1)}, u32[]{:S(2)}) copy-start(bf16[1,192,3072]{2,1,0:T(8,128)(2,1)} %param.25) | copy-start | bytes 3538948
  13.6 100.0 %copy-start.37 = (s32[1024]{0:T(1024)S(1)}, s32[1024]{0:T(1024)}, u32[]{:S(2)}) copy-start(s32[1024]{0:T(1024)} %param.29) | copy-start | bytes 12292
  13.6 101.7 %copy-start.12 = (bf16[1,128,768]{2,1,0:T(8,128)(2,1)S(1)}, bf16[1,128,768]{2,1,0:T(8,128)(2,1)}, u32[]{:S(2)}) copy-start(bf16[1,128,768]{2,1,0:T(8,128)(2,1)} %param.16) | copy-start | bytes 589828
  81.9 82.2 %copy-start.1 = (bf16[128,2304]{1,0:T(8,128)(2,1)}, bf16[128,2304]{1,0:T(8,128)(2,1)S(1)}, u32[]{:S(2)}) copy-start(bf16[128,2304]{1,0:T(8,128)(2,1)S(1)} %convolution_convert_fusion.3.q_ref.k_ref.v_ref) | copy-start | bytes 1769476
  81.9 33.8 %copy-start.30 = (s32[1,128,2]{1,2,0:T(2,128)S(1)}, s32[1,128,2]{1,2,0:T(2,128)}, u32[]{:S(2)}) copy-start(s32[1,128,2]{1,2,0:T(2,128)} %param.28) | copy-start | bytes 3076
  82.8 30.8 %collective-permute-start = (bf16[192,3072]{1,0:T(8,128)(2,1)S(1)}, bf16[192,3072]{1,0:T(8,128)(2,1)}, u32[]{:S(2)}, u32[]{:S(2)}) collective-permute-start(bf16[192,3072]{1,0:T(8,128)(2,1)S(1)} %bitcast.141), channel_id=1, source_target_pairs={{0,1},{1,2},{2,3},{3,0},{4,5},{5,6},{6,7},{7,4},{8,9},{9,10},{10,1... | collective-permute-start | bytes 3538952 | tf_op jit(solution)/shard_map/ppermute | solution.py:139
  84.7 54.1 %collective-permute-start.3 = (bf16[192,3072]{1,0:T(8,128)(2,1)}, bf16[192,3072]{1,0:T(8,128)(2,1)}, u32[]{:S(2)}, u32[]{:S(2)}) collective-permute-start(bf16[192,3072]{1,0:T(8,128)(2,1)} %bitcast.143), channel_id=1, source_target_pairs={{0,1},{1,2},{2,3},{3,0},{4,5},{5,6},{6,7},{7,4},{8,9},{9,10},{10,1... | collective-permute-start | bytes 3538952 | tf_op jit(solution)/shard_map/ppermute | solution.py:139
  113.5 50.6 %collective-permute-start.1 = (bf16[192,3072]{1,0:T(8,128)(2,1)}, bf16[192,3072]{1,0:T(8,128)(2,1)}, u32[]{:S(2)}, u32[]{:S(2)}) collective-permute-start(bf16[192,3072]{1,0:T(8,128)(2,1)} %collective-permute-done), channel_id=1, source_target_pairs={{0,1},{1,2},{2,3},{3,0},{4,5},{5,6},{6,7},{7,4},{8,9},{9,10},{10,1... | collective-permute-start | bytes 3538952 | tf_op jit(solution)/shard_map/ppermute | solution.py:139
  115.8 57.8 %copy-start.14 = (bf16[1,128,768]{2,1,0:T(8,128)(2,1)S(1)}, bf16[1,128,768]{2,1,0:T(8,128)(2,1)}, u32[]{:S(2)}) copy-start(bf16[1,128,768]{2,1,0:T(8,128)(2,1)} %param.15) | copy-start | bytes 589828
  115.8 60.2 %copy-start.23 = (f32[768]{0:T(1024)S(1)}, f32[768]{0:T(1024)}, u32[]{:S(2)}) copy-start(f32[768]{0:T(1024)} %param.23) | copy-start | bytes 9220
  138.8 50.6 %collective-permute-start.4 = (bf16[192,3072]{1,0:T(8,128)(2,1)}, bf16[192,3072]{1,0:T(8,128)(2,1)}, u32[]{:S(2)}, u32[]{:S(2)}) collective-permute-start(bf16[192,3072]{1,0:T(8,128)(2,1)} %collective-permute-done.3), channel_id=1, source_target_pairs={{0,1},{1,2},{2,3},{3,0},{4,5},{5,6},{6,7},{7,4},{8,9},{9,10},{10,1... | collective-permute-start | bytes 3538952 | tf_op jit(solution)/shard_map/ppermute | solution.py:139
  164.1 50.6 %collective-permute-start.2 = (bf16[192,3072]{1,0:T(8,128)(2,1)}, bf16[192,3072]{1,0:T(8,128)(2,1)}, u32[]{:S(2)}, u32[]{:S(2)}) collective-permute-start(bf16[192,3072]{1,0:T(8,128)(2,1)} %collective-permute-done.1), channel_id=1, source_target_pairs={{0,1},{1,2},{2,3},{3,0},{4,5},{5,6},{6,7},{7,4},{8,9},{9,10},{10,1... | collective-permute-start | bytes 3538952 | tf_op jit(solution)/shard_map/ppermute | solution.py:139
  180.7 18.2 %all-to-all-start = ((bf16[8,36,1536]{2,1,0:T(8,128)(2,1)}), bf16[8,36,1536]{2,1,0:T(8,128)(2,1)S(1)}, u32[]{:S(2)}, u32[]{:S(2)}) async-start(bf16[8,36,1536]{2,1,0:T(8,128)(2,1)} %reshape.257), calls=%async_computation | async-start | bytes 1966080 | tf_op jit(solution)/shard_map/all_to_all | solution.py:337
  189.4 49.9 %collective-permute-start.5 = (bf16[192,3072]{1,0:T(8,128)(2,1)}, bf16[192,3072]{1,0:T(8,128)(2,1)}, u32[]{:S(2)}, u32[]{:S(2)}) collective-permute-start(bf16[192,3072]{1,0:T(8,128)(2,1)} %collective-permute-done.4), channel_id=1, source_target_pairs={{0,1},{1,2},{2,3},{3,0},{4,5},{5,6},{6,7},{7,4},{8,9},{9,10},{10,1... | collective-permute-start | bytes 3538952 | tf_op jit(solution)/shard_map/ppermute | solution.py:139
  199.1 19.9 %copy-start.9 = (bf16[288,1536]{1,0:T(8,128)(2,1)}, bf16[288,1536]{1,0:T(8,128)(2,1)S(1)}, u32[]{:S(2)}) copy-start(bf16[288,1536]{1,0:T(8,128)(2,1)S(1)} %reshape.258) | copy-start | bytes 2654212
  199.1 40.2 %copy-start.63 = (bf16[1,3072,192]{1,2,0:T(8,128)(2,1)S(1)}, bf16[1,3072,192]{1,2,0:T(8,128)(2,1)}, u32[]{:S(2)}) copy-start(bf16[1,3072,192]{1,2,0:T(8,128)(2,1)} %param.26) | copy-start | bytes 3538948
  252.8 19.0 %all-to-all-start.1 = ((bf16[8,36,1536]{2,1,0:T(8,128)(2,1)}), bf16[8,36,1536]{2,1,0:T(8,128)(2,1)}, u32[]{:S(2)}, u32[]{:S(2)}) async-start(bf16[8,36,1536]{2,1,0:T(8,128)(2,1)} %reshape.259), calls=%async_computation.1 | async-start | bytes 1966080 | tf_op jit(solution)/shard_map/all_to_all | solution.py:350
  257.1 77.1 %all-gather.12.cloned.1.call-start = ((), (), s32[]{:S(2)}) async-start(), calls=%async_computation.7 | async-start | bytes 2064384 | tf_op jit(solution)/shard_map/all_gather | solution.py:391
  304.0 50.8 %all-gather.10.cloned.1.call-start = ((), (), s32[]{:S(2)}) async-start(), calls=%async_computation.6 | async-start | bytes 1769472 | tf_op jit(solution)/shard_map/all_gather | solution.py:268
  305.7 174.6 %reduce-scatter.3.cloned.1.call-start = ((), (), s32[]{:S(2)}) async-start(), calls=%async_computation.8 | async-start | bytes 5308416 | tf_op jit(solution)/shard_map/reduce_scatter | solution.py:422
  369.4 147.4 %reduce-scatter.5.cloned.1.call-start = ((), (), s32[]{:S(2)}) async-start(), calls=%async_computation.9 | async-start | bytes 737280 | tf_op jit(solution)/shard_map/reduce_scatter | solution.py:423
  372.3 30.9 %collective-permute-start.6 = (bf16[192,3072]{1,0:T(8,128)(2,1)}, bf16[192,3072]{1,0:T(8,128)(2,1)}, u32[]{:S(2)}, u32[]{:S(2)}) collective-permute-start(bf16[192,3072]{1,0:T(8,128)(2,1)} %convolution_convert_fusion.2), channel_id=1, source_target_pairs={{0,1},{1,2},{2,3},{3,0},{4,5},{5,6},{6,7},{7,4},{8,9},{9,10},{10,1... | collective-permute-start | bytes 3538952 | tf_op jit(solution)/shard_map/ppermute | solution.py:139
  376.7 51.8 %collective-permute-start.9 = (bf16[192,3072]{1,0:T(8,128)(2,1)}, bf16[192,3072]{1,0:T(8,128)(2,1)}, u32[]{:S(2)}, u32[]{:S(2)}) collective-permute-start(bf16[192,3072]{1,0:T(8,128)(2,1)} %convolution_convert_fusion.1), channel_id=1, source_target_pairs={{0,1},{1,2},{2,3},{3,0},{4,5},{5,6},{6,7},{7,4},{8,9},{9,10},{10,1... | collective-permute-start | bytes 3538952 | tf_op jit(solution)/shard_map/ppermute | solution.py:139
  379.5 23.7 %copy-start.10 = (bf16[288,1536]{1,0:T(8,128)(2,1)S(1)}, bf16[288,1536]{1,0:T(8,128)(2,1)}, u32[]{:S(2)}) copy-start(bf16[288,1536]{1,0:T(8,128)(2,1)} %copy-done.9) | copy-start | bytes 2654212
  405.3 48.4 %collective-permute-start.7 = (bf16[192,3072]{1,0:T(8,128)(2,1)S(1)}, bf16[192,3072]{1,0:T(8,128)(2,1)S(1)}, u32[]{:S(2)}, u32[]{:S(2)}) collective-permute-start(bf16[192,3072]{1,0:T(8,128)(2,1)S(1)} %add_convert_fusion.3), channel_id=1, source_target_pairs={{0,1},{1,2},{2,3},{3,0},{4,5},{5,6},{6,7},{7,4},{8,9},{9,10},{10,1... | collective-permute-start | bytes 3538952 | tf_op jit(solution)/shard_map/ppermute | solution.py:139
  430.6 48.4 %collective-permute-start.10 = (bf16[192,3072]{1,0:T(8,128)(2,1)S(1)}, bf16[192,3072]{1,0:T(8,128)(2,1)S(1)}, u32[]{:S(2)}, u32[]{:S(2)}) collective-permute-start(bf16[192,3072]{1,0:T(8,128)(2,1)S(1)} %add_convert_fusion.1), channel_id=1, source_target_pairs={{0,1},{1,2},{2,3},{3,0},{4,5},{5,6},{6,7},{7,4},{8,9},{9,10},{10,1... | collective-permute-start | bytes 3538952 | tf_op jit(solution)/shard_map/ppermute | solution.py:139
  455.0 25.4 %copy-start.4 = (f32[128,768]{1,0:T(8,128)S(1)}, f32[128,768]{1,0:T(8,128)}, u32[]{:S(2)}) copy-start(f32[128,768]{1,0:T(8,128)} %copy-done.2) | copy-start | bytes 1179652
  455.0 25.4 %copy-start.25 = (f32[128,8]{0,1:T(8,128)S(1)}, f32[128,8]{0,1:T(8,128)}, u32[]{:S(2)}) copy-start(f32[128,8]{0,1:T(8,128)} %copy-done.24) | copy-start | bytes 12292
  455.0 25.4 %copy-start.34 = (f32[128]{0:T(128)S(1)}, f32[128]{0:T(128)}, u32[]{:S(2)}) copy-start(f32[128]{0:T(128)} %copy-done.32) | copy-start | bytes 1540
  455.0 25.4 %copy-start.40 = (f32[128]{0:T(128)S(1)}, f32[128]{0:T(128)}, u32[]{:S(2)}) copy-start(f32[128]{0:T(128)} %copy-done.38) | copy-start | bytes 1540
  455.0 25.4 %copy-start.49 = (f32[128]{0:T(128)S(1)}, f32[128]{0:T(128)}, u32[]{:S(2)}) copy-start(f32[128]{0:T(128)} %copy-done.47) | copy-start | bytes 1540
  455.0 25.4 %copy-start.54 = (f32[128]{0:T(128)S(1)}, f32[128]{0:T(128)}, u32[]{:S(2)}) copy-start(f32[128]{0:T(128)} %copy-done.53) | copy-start | bytes 1540
  455.0 26.5 %copy-start.26 = (f32[6,2,1152]{2,1,0:T(2,128)S(1)}, f32[6,2,1152]{2,1,0:T(2,128)}, u32[]{:S(2)}) copy-start(f32[6,2,1152]{2,1,0:T(2,128)} %get-tuple-element.25) | copy-start | bytes 165892
  455.0 26.5 %copy-start.29 = (s32[1152]{0:T(1024)S(1)}, s32[1152]{0:T(1024)}, u32[]{:S(2)}) copy-start(s32[1152]{0:T(1024)} %dynamic_slice.59) | copy-start | bytes 13828
  455.0 58.8 %copy-start.5 = (f32[192,3072]{1,0:T(8,128)S(1)}, f32[192,3072]{1,0:T(8,128)}, u32[]{:S(2)}) copy-start(f32[192,3072]{1,0:T(8,128)} %fusion.60) | copy-start | bytes 7077892
  455.0 58.8 %collective-permute-start.8 = (bf16[192,3072]{1,0:T(8,128)(2,1)}, bf16[192,3072]{1,0:T(8,128)(2,1)}, u32[]{:S(2)}, u32[]{:S(2)}) collective-permute-start(bf16[192,3072]{1,0:T(8,128)(2,1)} %add_convert_fusion.2), channel_id=1, source_target_pairs={{0,1},{1,2},{2,3},{3,0},{4,5},{5,6},{6,7},{7,4},{8,9},{9,10},{10,1... | collective-permute-start | bytes 3538952 | tf_op jit(solution)/shard_map/ppermute | solution.py:139
  480.3 58.2 %collective-permute-start.11 = (bf16[192,3072]{1,0:T(8,128)(2,1)}, bf16[192,3072]{1,0:T(8,128)(2,1)}, u32[]{:S(2)}, u32[]{:S(2)}) collective-permute-start(bf16[192,3072]{1,0:T(8,128)(2,1)} %add_convert_fusion), channel_id=1, source_target_pairs={{0,1},{1,2},{2,3},{3,0},{4,5},{5,6},{6,7},{7,4},{8,9},{9,10},{10,1... | collective-permute-start | bytes 3538952 | tf_op jit(solution)/shard_map/ppermute | solution.py:139
  480.3 107.0 %all-gather.14.cloned.1.call-start = ((), (), s32[]{:S(2)}) async-start(), calls=%async_computation.10 | async-start | bytes 1327104 | tf_op jit(solution)/shard_map/all_gather | solution.py:424
  516.9 25.3 %copy-start.15 = (bf16[1,128,768]{2,1,0:T(8,128)(2,1)S(1)}, bf16[1,128,768]{2,1,0:T(8,128)(2,1)}, u32[]{:S(2)}) copy-start(bf16[1,128,768]{2,1,0:T(8,128)(2,1)} %param.15) | copy-start | bytes 589828
  516.9 25.3 %copy-start.20 = (bf16[128,2304]{1,0:T(8,128)(2,1)S(1)}, bf16[128,2304]{1,0:T(8,128)(2,1)}, u32[]{:S(2)}) copy-start(bf16[128,2304]{1,0:T(8,128)(2,1)} %copy-done.19) | copy-start | bytes 1769476
  516.9 25.3 %copy-start.35 = (f32[768]{0:T(1024)S(1)}, f32[768]{0:T(1024)}, u32[]{:S(2)}) copy-start(f32[768]{0:T(1024)} %param.17) | copy-start | bytes 9220
  516.9 25.3 %copy-start.56 = (f32[128]{0:T(128)S(1)}, f32[128]{0:T(128)}, u32[]{:S(2)}) copy-start(f32[128]{0:T(128)} %copy-done.55) | copy-start | bytes 1540
  542.2 44.1 %copy-start.58 = (f32[128]{0:T(128)S(1)}, f32[128]{0:T(128)}, u32[]{:S(2)}) copy-start(f32[128]{0:T(128)} %copy-done.57) | copy-start | bytes 1540
  542.2 44.1 %copy-start.8 = (f32[128,768]{1,0:T(8,128)S(1)}, f32[128,768]{1,0:T(8,128)}, u32[]{:S(2)}) copy-start(f32[128,768]{1,0:T(8,128)} %copy-done.6) | copy-start | bytes 1179652
  (39 other events, 103.1 us)
Sparse Core Ops, SparseCore 0:
  12.0 67.0 all-gather.5
  82.9 31.1 all-gather.7
  304.1 23.1 all-gather.11
  329.0 25.6 all-gather.9
  369.5 53.8 reduce-scatter.2
  480.4 30.2 reduce-scatter.4
  517.0 22.2 all-gather.13

commit v3 on v2

--- a/solution.py
+++ b/solution.py
@@ -146,14 +146,12 @@
     return blocks
 
 
-def ring_sum(term, count):
-    running = term(1).astype(jnp.bfloat16) if count > 1 else None
+def ring_hops(term, count):
+    hops = [ring_step(term(1).astype(jnp.bfloat16), count)]
     for place in range(2, count):
-        arrived = ring_step(running, count).astype(jnp.float32)
-        running = (arrived + term(place)).astype(jnp.bfloat16)
-    if count == 1:
-        return term(0)
-    return ring_step(running, count).astype(jnp.float32) + term(0)
+        running = (hops[-1].astype(jnp.float32) + term(place)).astype(jnp.bfloat16)
+        hops.append(ring_step(running, count))
+    return hops
 
 
 def split_three(values):
@@ -200,8 +198,6 @@
     share = part_rows // lines
     first_blocks = ring_blocks(w_in[0], part_count)
     second_blocks = ring_blocks(w_out[0].T, part_count)
-    first_weight = jnp.concatenate(first_blocks, axis=0)
-    second_turned = jnp.concatenate(second_blocks, axis=0)
 
     def my_share(matrix):
         return lax.dynamic_slice_in_dim(matrix, my_index * share, share, 0)
@@ -217,6 +213,9 @@
         axis=1,
     )
     mixer_all = lax.all_gather(mixer_share, ("dp", "expert"), axis=0, tiled=True)
+    mixer_all, first_blocks[1], second_blocks[1] = lax.optimization_barrier(
+        (mixer_all, first_blocks[1], second_blocks[1])
+    )
     wqkv_all = mixer_all[:, : 3 * model_width]
     output_all = mixer_all[:, 3 * model_width : 4 * model_width]
     router = mixer_all[:, 4 * model_width : 4 * model_width + experts].astype(jnp.float32)
@@ -265,6 +264,9 @@
     normed1 = normed1_f.astype(jnp.bfloat16)
     projected = jnp.dot(normed1, wqkv_all, preferred_element_type=jnp.float32).astype(jnp.bfloat16)
     mixed_all = lax.all_gather(projected[:, model_width:], "expert", axis=0, tiled=True)
+    mixed_all, first_blocks[2] = lax.optimization_barrier((mixed_all, first_blocks[2]))
+    first_weight = jnp.concatenate(first_blocks, axis=0)
+    second_turned = jnp.concatenate(second_blocks, axis=0)
     queries_all = lax.all_gather(projected[:, :model_width], "expert", axis=0, tiled=True)
     pair_cost = 2 * tok_rows * seq_len * model_width
     mixer_specs = [
@@ -337,6 +339,7 @@
     received = lax.all_to_all(
         outgoing, "expert", split_axis=0, concat_axis=0, tiled=True
     ).reshape(slots, 2 * model_width)
+    received, queries_all = lax.optimization_barrier((received, queries_all))
     arrived = received[:, :model_width]
     grad_arrived = received[:, model_width:]
     pre_act = jnp.dot(arrived, first_weight, preferred_element_type=jnp.float32)
@@ -365,10 +368,14 @@
     def feature_block(values, place):
         return values[:, place * part_rows : (place + 1) * part_rows]
 
-    first_sum = ring_sum(lambda place: outer(feature_block(arrived, place), grad_pre), part_count)
-    second_sum = ring_sum(
-        lambda place: outer(feature_block(grad_arrived, place), activated), part_count
-    )
+    def first_term(place):
+        return outer(feature_block(arrived, place), grad_pre)
+
+    def second_term(place):
+        return outer(feature_block(grad_arrived, place), activated)
+
+    first_hops = ring_hops(first_term, part_count)
+    second_hops = ring_hops(second_term, part_count)
     back = jnp.dot(placing, returned, preferred_element_type=jnp.float32).astype(jnp.bfloat16)
     made_back = turn(back[:, :model_width]).astype(jnp.float32)
     rows_back = turn(back[:, model_width:]).astype(jnp.float32)
@@ -389,6 +396,9 @@
     stats = jnp.pad(stats, ((0, 0), (0, LANES - stats.shape[1])))
     packed = jnp.concatenate([grad_attended, stats], axis=1)
     packed_all = lax.all_gather(packed, "expert", axis=0, tiled=True)
+    packed_all, *_ = lax.optimization_barrier(
+        (packed_all, first_hops[0], second_hops[0], first_hops[1])
+    )
     grad_query_low, diagonals = pair_call(
         query_grad_kernel,
         pairs,
@@ -418,10 +428,6 @@
     )(projected, projected, queries_all, packed_all, line_turned, stats_all)
     grads_low = jnp.concatenate([grad_query_low, grad_keys, grad_values], axis=1)
     grad_qkv = outer(by_line(normed1), grads_low).astype(jnp.bfloat16)
-    grad_mixer = jnp.concatenate([grad_qkv, grad_output], axis=1)
-    line_sum = lax.psum_scatter(grad_mixer, "expert", scatter_dimension=0, tiled=True)
-    part_sum = lax.psum_scatter(line_sum, "dp", scatter_dimension=0, tiled=True)
-    matrix_sums = lax.all_gather(part_sum, "expert", axis=0, tiled=True).astype(jnp.float32)
     grad_normed1 = dot_nt(grads_low, wqkv_all)
     grad_inputs, grad_gain_one = norm1_back(grad_normed1)
     grad_hidden = (grad_resid + grad_inputs)[None]
@@ -434,10 +440,17 @@
         (((1,), (1,)), ((), ())),
         precision=HIGHEST,
     )
+    grad_mixer = jnp.concatenate([grad_qkv, grad_output], axis=1)
+    line_sum = lax.psum_scatter(grad_mixer, "expert", scatter_dimension=0, tiled=True)
     small = jnp.concatenate(
         [grad_gain_one, grad_gain_two, grad_table.reshape(-1), grad_router.reshape(-1)]
     )
     small = lax.psum(small, ("dp", "expert"))
+    line_sum, small = lax.optimization_barrier((line_sum, small))
+    part_sum = lax.psum_scatter(line_sum, "dp", scatter_dimension=0, tiled=True)
+    matrix_sums = lax.all_gather(part_sum, "expert", axis=0, tiled=True).astype(jnp.float32)
+    first_sum = first_hops[-1].astype(jnp.float32) + first_term(0)
+    second_sum = second_hops[-1].astype(jnp.float32) + second_term(0)
 
     def mine(values):
         size = values.shape[0] // part_count
@@ -455,8 +468,8 @@
         mine(small[2 * model_width : table_end].reshape(bucket_count, head_count)),
         mine(small[model_width : 2 * model_width]),
         mine(small[table_end:].reshape(model_width, experts)),
-        first_sum.astype(jnp.float32)[None],
-        second_sum.astype(jnp.float32).T[None],
+        first_sum[None],
+        second_sum.T[None],
     )
 
 

time: 599 us -> 547 us (0.913)
  waiting for transfers between devices: 347 us -> 254 us
  blocking collectives: 37.7 us -> 60 us
  matrix products: 53 us -> 64.3 us
    ppermute x12, waiting for transfers between devices: 257 us -> 166 us  [ring_step(): lax.ppermute(values, 'dp', [(part, (part + 1) % count) for part in range(...]
    all_gather x1, waiting for transfers between devices: 65.5 us -> 43 us  [on_device(): lax.all_gather(mixer_share, ('dp', 'expert'), axis=0, tiled=True)]
    psum x1, blocking collectives: 37.7 us -> 60 us  [on_device(): small = lax.psum(small, ('dp', 'expert'))]
    reduce_scatter x1, waiting for transfers between devices: 0.01 us -> 20.9 us  [on_device(): part_sum = lax.psum_scatter(line_sum, 'dp', scatter_dimension=0, tiled=True)]
    all_gather x1, waiting for transfers between devices: 10.1 us -> 0.02 us  [on_device(): lax.all_gather(projected[:, :model_width], 'expert', axis=0, tiled=True)]
    dot_general x10, matrix products: 19.7 us -> 27.6 us  [outer(): lax.dot_general(left, right, (((0,), (0,)), ((), ())), preferred_element_...]
    all_gather x1, waiting for transfers between devices: 0.01 us -> 6.79 us  [on_device(): lax.all_gather(part_sum, 'expert', axis=0, tiled=True).astype(jnp.float32)]
    unnamed x141 -> x151, local copies, waits for them, and re-layouts: 12.4 us -> 11.8 us
  transfers between devices with their start and end apart: 21 -> 21, of which waited for: 16 -> 14; matrix products, arithmetic and copies ran while one was open for 15% -> 17% of each run, Pallas kernels for 4% -> 4%
where the time goes in v3:
time: 547 us; the launch traced here: 544 us
  waiting for transfers between devices  254 us (46%)
  local copies, waits for them, and re-layouts  66 us (12%)
  matrix products  64.3 us (12%)
  blocking collectives  60 us (11%)
  other arithmetic  37.6 us (7%)
  Pallas kernels  29.2 us (5%)
  starting transfers between devices  17.6 us (3%)
  between operations  15.3 us (3%)
    ppermute x12, waiting for transfers between devices, ring_step(): lax.ppermute(values, 'dp', [(part, (part + 1) % count) for part in range(...  166 us
    psum x1, blocking collectives, on_device(): small = lax.psum(small, ('dp', 'expert'))  60 us
    all_gather x1, waiting for transfers between devices, on_device(): lax.all_gather(mixer_share, ('dp', 'expert'), axis=0, tiled=True)  43 us
    dot_general x10, matrix products, outer(): lax.dot_general(left, right, (((0,), (0,)), ((), ())), preferred_element_...  27.6 us
    reduce_scatter x1, waiting for transfers between devices, on_device(): part_sum = lax.psum_scatter(line_sum, 'dp', scatter_dimension=0, tiled=True)  20.9 us
    dot_general x4, matrix products, dot_nt(): lax.dot_general(left, right, (((1,), (1,)), ((), ())), preferred_element_...  13.7 us
    all_to_all x1, waiting for transfers between devices, on_device(): lax.all_to_all(outgoing, 'expert', split_axis=0, concat_axis=0, tiled=True)  13 us
    pallas_call x1, Pallas kernels, on_device(): pair_call(query_grad_kernel, pairs, mixer_specs + [columns(tok_rows, 0)]...  11.9 us
  transfers between devices with their start and end apart: 21, of which 14 were waited for; matrix products, arithmetic and copies ran while one was open for 17% of the time, Pallas kernels for 4%

profile of v3, /device:TPU:0, one launch (start us, length us, event | category | flops | bytes accessed | tf_op | source)
XLA Modules:
  0.0 544.2 jit_solution(944131357732169372)
XLA Ops:
  11.9 3.1 collective-permute-start
  18.2 29.2 %collective-permute-done = bf16[192,3072]{1,0:T(8,128)(2,1)} collective-permute-done((bf16[192,3072]{1,0:T(8,128)(2,1)}, bf16[192,3072]{1,0:T(8,128)(2,1)}, u32[]{:S(2)}, u32[]{:S(2)}) %collective-permute-start) | collective-permute-done | bytes 1179680 | tf_op jit(solution)/shard_map/ppermute | solution.py:139
  47.5 24.3 %collective-permute-done.1 = bf16[192,3072]{1,0:T(8,128)(2,1)S(1)} collective-permute-done((bf16[192,3072]{1,0:T(8,128)(2,1)}, bf16[192,3072]{1,0:T(8,128)(2,1)S(1)}, u32[]{:S(2)}, u32[]{:S(2)}) %collective-permute-start.1) | collective-permute-done | bytes 1179680 | tf_op jit(solution)/shard_map/ppermute | solution.py:139
  71.8 43.0 %all-gather.6.cloned.1.call-done = bf16[768,3200]{1,0:T(8,128)(2,1)} async-done(((bf16[24,3200]{1,0:T(8,128)(2,1)}), bf16[768,3200]{1,0:T(8,128)(2,1)}) %all-gather.6.cloned.1.call-update) | async-done | bytes 4915216 | tf_op jit(solution)/shard_map/all_gather | solution.py:215
  114.9 2.8 convolution_convert_fusion.3.q_ref.k_ref.v_ref
  118.6 1.9 collective-permute-start.2
  123.5 26.0 %collective-permute-done.2 = bf16[192,3072]{1,0:T(8,128)(2,1)} collective-permute-done((bf16[192,3072]{1,0:T(8,128)(2,1)}, bf16[192,3072]{1,0:T(8,128)(2,1)}, u32[]{:S(2)}, u32[]{:S(2)}) %collective-permute-start.2) | collective-permute-done | bytes 1179680 | tf_op jit(solution)/shard_map/ppermute | solution.py:139
  150.4 9.4 %shard_map.238 = (bf16[128,768]{1,0:T(8,128)(2,1)}, f32[128,768]{1,0:T(8,128)}, f32[128,768]{1,0:T(8,128)}) custom-call(bf16[128,2304]{1,0:T(8,128)(2,1)} %copy-done.1, bf16[1024,1536]{1,0:T(8,128)(2,1)} %all-gather.8.cloned.1.call-done.k_ref.v_ref, bf16[1024,1536]{1,0:T(8,128)(2,1)} %all-gather.8.cloned.1.call-done.k_ref.v_ref, f32[6,2,1152]{2,1,0:T(2,128)} %reshape.256.line_ref), custom_call_target="tpu_custom_call" | custom-call | flops 603979776 | bytes 6039797 | tf_op jit(solution)/shard_map/pallas_call | solution.py:280
  166.6 3.6 all-to-all-start
  170.1 4.7 collective-permute-done.4
  174.9 13.0 %all-to-all-done = bf16[8,36,1536]{2,1,0:T(8,128)(2,1)S(1)} async-done(((bf16[8,36,1536]{2,1,0:T(8,128)(2,1)}), bf16[8,36,1536]{2,1,0:T(8,128)(2,1)S(1)}, u32[]{:S(2)}, u32[]{:S(2)}) %all-to-all-start) | async-done | bytes 884768 | tf_op jit(solution)/shard_map/all_to_all | solution.py:339
  188.1 12.0 %collective-permute-done.3 = bf16[192,3072]{1,0:T(8,128)(2,1)} collective-permute-done((bf16[192,3072]{1,0:T(8,128)(2,1)}, bf16[192,3072]{1,0:T(8,128)(2,1)}, u32[]{:S(2)}, u32[]{:S(2)}) %collective-permute-start.3) | collective-permute-done | bytes 1179680 | tf_op jit(solution)/shard_map/ppermute | solution.py:139
  200.1 4.3 multiply_convert_fusion
  204.4 20.3 %collective-permute-done.5 = bf16[192,3072]{1,0:T(8,128)(2,1)} collective-permute-done((bf16[192,3072]{1,0:T(8,128)(2,1)}, bf16[192,3072]{1,0:T(8,128)(2,1)}, u32[]{:S(2)}, u32[]{:S(2)}) %collective-permute-start.5) | collective-permute-done | bytes 1179680 | tf_op jit(solution)/shard_map/ppermute | solution.py:139
  224.7 3.7 fusion
  228.4 3.3 convolution_convert_fusion.7
  231.8 3.2 convolution_convert_fusion.8
  235.9 2.2 reshape.259
  238.1 4.3 all-to-all-start.1
  252.8 4.2 all-to-all-done.1
  257.1 2.2 reshape.260
  262.2 2.3 concatenate.89
  264.5 2.4 concatenate.88
  269.2 2.1 multiply_reduce_fusion.2
  272.8 2.6 convert_multiply_fusion
  289.4 2.8 convolution_convert_fusion.2
  292.3 2.9 convolution_convert_fusion.1
  296.0 27.2 %collective-permute-done.6 = bf16[192,3072]{1,0:T(8,128)(2,1)} collective-permute-done((bf16[192,3072]{1,0:T(8,128)(2,1)}, bf16[192,3072]{1,0:T(8,128)(2,1)}, u32[]{:S(2)}, u32[]{:S(2)}) %collective-permute-start.6) | collective-permute-done | bytes 1179680 | tf_op jit(solution)/shard_map/ppermute | solution.py:139
  323.2 3.2 add_convert_fusion.3
  339.2 11.9 %shard_map.239 = (bf16[128,768]{1,0:T(8,128)(2,1)}, f32[6,2,1152]{2,1,0:T(2,128)}) custom-call(bf16[128,2304]{1,0:T(8,128)(2,1)} %copy-done.1, bf16[1024,1536]{1,0:T(8,128)(2,1)} %all-gather.8.cloned.1.call-done.k_ref.v_ref, bf16[1024,1536]{1,0:T(8,128)(2,1)} %all-gather.8.cloned.1.call-done.k_ref.v_ref, f32[6,2,1152]{2,1,0:T(2,128)} %reshape.256.line_ref, ...), custom_call_target="tpu_custom_call" | custom-call | flops 1006632960 | bytes 10066329 | tf_op jit(solution)/shard_map/pallas_call | solution.py:402
  354.1 15.5 %collective-permute-done.8 = bf16[192,3072]{1,0:T(8,128)(2,1)} collective-permute-done((bf16[192,3072]{1,0:T(8,128)(2,1)}, bf16[192,3072]{1,0:T(8,128)(2,1)}, u32[]{:S(2)}, u32[]{:S(2)}) %collective-permute-start.8) | collective-permute-done | bytes 1179680 | tf_op jit(solution)/shard_map/ppermute | solution.py:139
  371.4 1.9 copy.65
  380.1 7.9 %shard_map.240 = (bf16[128,768]{1,0:T(8,128)(2,1)}, bf16[128,768]{1,0:T(8,128)(2,1)}) custom-call(bf16[128,2304]{1,0:T(8,128)(2,1)} %copy-done.1, bf16[128,2304]{1,0:T(8,128)(2,1)} %copy-done.1, bf16[1024,768]{1,0:T(8,128)(2,1)} %all-gather.10.cloned.1.call-done.q_ref, bf16[1024,896]{1,0:T(8,128)(2,1)} %all-gather.12.cloned.1.call-done.grad_ref, ...), custom_call_target="tpu_custom_call" | custom-call | flops 805306368 | bytes 8053063 | tf_op jit(solution)/shard_map/pallas_call | solution.py:414
  391.9 2.8 pad_maximum_fusion.2
  396.4 3.2 fusion.53
  399.6 3.3 add_convert_fusion.1
  410.5 3.4 add_convert_fusion.2
  413.9 4.6 fusion.31
  419.1 60.0 %psum.7 = f32[8064]{0:T(1024)} all-reduce(f32[8064]{0:T(1024)} %pad_maximum_fusion.9), channel_id=1, replica_groups=mesh['expert'=8,'dp'=4] {'dp','expert'}, use_global_device_ids=true, to_apply=%region_20.21 | all-reduce | flops 8064 | bytes 64512 | tf_op jit(solution)/shard_map/psum | solution.py:448
  479.2 3.3 add_convert_fusion
  483.2 3.1 fusion.59
  486.3 3.1 fusion.51
  489.4 20.9 %reduce-scatter.5.cloned.1.call-done = bf16[24,3072]{1,0:T(8,128)(2,1)} async-done(((bf16[96,3072]{1,0:T(8,128)(2,1)}), bf16[24,3072]{1,0:T(8,128)(2,1)}) %reduce-scatter.5.cloned.1.call-update) | async-done | bytes 147472 | tf_op jit(solution)/shard_map/reduce_scatter | solution.py:450
  510.3 3.9 add_bitcast_fusion.1
  514.2 6.9 %collective-permute-done.11 = bf16[192,3072]{1,0:T(8,128)(2,1)} collective-permute-done((bf16[192,3072]{1,0:T(8,128)(2,1)}, bf16[192,3072]{1,0:T(8,128)(2,1)}, u32[]{:S(2)}, u32[]{:S(2)}) %collective-permute-start.11) | collective-permute-done | bytes 1179680 | tf_op jit(solution)/shard_map/ppermute | solution.py:139
  521.2 2.9 add_bitcast_fusion
  527.9 6.8 %all-gather.14.cloned.1.call-done = bf16[192,3072]{1,0:T(8,128)(2,1)} async-done(((bf16[24,3072]{1,0:T(8,128)(2,1)}), bf16[192,3072]{1,0:T(8,128)(2,1)}) %all-gather.14.cloned.1.call-update) | async-done | bytes 1179664 | tf_op jit(solution)/shard_map/all_gather | solution.py:451
  534.7 2.7 fusion.101
  (295 shorter events, 94.6 us)
Async XLA Ops:
  7.2 114.1 %copy-start = (f32[32,12]{0,1:T(8,128)S(1)}, f32[32,12]{0,1:T(8,128)}, u32[]{:S(2)}) copy-start(f32[32,12]{0,1:T(8,128)} %param.22) | copy-start | bytes 4612
  7.2 107.7 %all-gather.6.cloned.1.call-start = ((), (), s32[]{:S(2)}) async-start(), calls=%async_computation.4 | async-start | bytes 5068800 | tf_op jit(solution)/shard_map/all_gather | solution.py:215
  11.9 138.5 %all-gather.8.cloned.1.call-start = ((), (), s32[]{:S(2)}) async-start(), calls=%async_computation.5 | async-start | bytes 3538944 | tf_op jit(solution)/shard_map/all_gather | solution.py:266
  11.9 35.5 %collective-permute-start = (bf16[192,3072]{1,0:T(8,128)(2,1)}, bf16[192,3072]{1,0:T(8,128)(2,1)}, u32[]{:S(2)}, u32[]{:S(2)}) collective-permute-start(bf16[192,3072]{1,0:T(8,128)(2,1)} %bitcast.140), channel_id=1, source_target_pairs={{0,1},{1,2},{2,3},{3,0},{4,5},{5,6},{6,7},{7,4},{8,9},{9,10},{10,1... | collective-permute-start | bytes 3538952 | tf_op jit(solution)/shard_map/ppermute | solution.py:139
  15.0 56.8 %collective-permute-start.1 = (bf16[192,3072]{1,0:T(8,128)(2,1)}, bf16[192,3072]{1,0:T(8,128)(2,1)S(1)}, u32[]{:S(2)}, u32[]{:S(2)}) collective-permute-start(bf16[192,3072]{1,0:T(8,128)(2,1)} %bitcast.143), channel_id=1, source_target_pairs={{0,1},{1,2},{2,3},{3,0},{4,5},{5,6},{6,7},{7,4},{8,9},{9,10},{10,1... | collective-permute-start | bytes 3538952 | tf_op jit(solution)/shard_map/ppermute | solution.py:139
  18.2 99.5 %copy-start.58 = (f32[128]{0:T(128)}, f32[128]{0:T(128)S(1)}, u32[]{:S(2)}) copy-start(f32[128]{0:T(128)S(1)} %fusion.93) | copy-start | bytes 1540
  18.2 102.3 %copy-start.39 = (s32[1024]{0:T(1024)S(1)}, s32[1024]{0:T(1024)}, u32[]{:S(2)}) copy-start(s32[1024]{0:T(1024)} %param.29) | copy-start | bytes 12292
  18.2 104.0 %copy-start.11 = (bf16[1,128,768]{2,1,0:T(8,128)(2,1)S(1)}, bf16[1,128,768]{2,1,0:T(8,128)(2,1)}, u32[]{:S(2)}) copy-start(bf16[1,128,768]{2,1,0:T(8,128)(2,1)} %param.16) | copy-start | bytes 589828
  71.8 50.8 %copy-start.66 = (bf16[192,3072]{1,0:T(8,128)(2,1)}, bf16[192,3072]{1,0:T(8,128)(2,1)S(1)}, u32[]{:S(2)}) copy-start(bf16[192,3072]{1,0:T(8,128)(2,1)S(1)} %collective-permute-done.1) | copy-start | bytes 3538948
  117.7 32.7 %copy-start.1 = (bf16[128,2304]{1,0:T(8,128)(2,1)}, bf16[128,2304]{1,0:T(8,128)(2,1)S(1)}, u32[]{:S(2)}) copy-start(bf16[128,2304]{1,0:T(8,128)(2,1)S(1)} %convolution_convert_fusion.3.q_ref.k_ref.v_ref) | copy-start | bytes 1769476
  117.7 4.9 copy-start.32
  118.5 69.6 %all-gather.10.cloned.1.call-start = ((), (), s32[]{:S(2)}) async-start(), calls=%async_computation.6 | async-start | bytes 1769472 | tf_op jit(solution)/shard_map/all_gather | solution.py:270
  118.6 31.0 %collective-permute-start.2 = (bf16[192,3072]{1,0:T(8,128)(2,1)}, bf16[192,3072]{1,0:T(8,128)(2,1)}, u32[]{:S(2)}, u32[]{:S(2)}) collective-permute-start(bf16[192,3072]{1,0:T(8,128)(2,1)} %collective-permute-done), channel_id=1, source_target_pairs={{0,1},{1,2},{2,3},{3,0},{4,5},{5,6},{6,7},{7,4},{8,9},{9,10},{10,1... | collective-permute-start | bytes 3538952 | tf_op jit(solution)/shard_map/ppermute | solution.py:139
  122.7 52.1 %collective-permute-start.4 = (bf16[192,3072]{1,0:T(8,128)(2,1)S(1)}, bf16[192,3072]{1,0:T(8,128)(2,1)}, u32[]{:S(2)}, u32[]{:S(2)}) collective-permute-start(bf16[192,3072]{1,0:T(8,128)(2,1)S(1)} %collective-permute-done.1), channel_id=1, source_target_pairs={{0,1},{1,2},{2,3},{3,0},{4,5},{5,6},{6,7},{7,4},{8,9},{9,10},{10,1... | collective-permute-start | bytes 3538952 | tf_op jit(solution)/shard_map/ppermute | solution.py:139
  149.5 50.6 %collective-permute-start.3 = (bf16[192,3072]{1,0:T(8,128)(2,1)}, bf16[192,3072]{1,0:T(8,128)(2,1)}, u32[]{:S(2)}, u32[]{:S(2)}) collective-permute-start(bf16[192,3072]{1,0:T(8,128)(2,1)} %collective-permute-done.2), channel_id=1, source_target_pairs={{0,1},{1,2},{2,3},{3,0},{4,5},{5,6},{6,7},{7,4},{8,9},{9,10},{10,1... | collective-permute-start | bytes 3538952 | tf_op jit(solution)/shard_map/ppermute | solution.py:139
  150.3 9.5 %copy-start.13 = (bf16[1,128,768]{2,1,0:T(8,128)(2,1)S(1)}, bf16[1,128,768]{2,1,0:T(8,128)(2,1)}, u32[]{:S(2)}) copy-start(bf16[1,128,768]{2,1,0:T(8,128)(2,1)} %param.15) | copy-start | bytes 589828
  150.3 11.4 %copy-start.25 = (f32[768]{0:T(1024)S(1)}, f32[768]{0:T(1024)}, u32[]{:S(2)}) copy-start(f32[768]{0:T(1024)} %param.23) | copy-start | bytes 9220
  166.6 21.3 %all-to-all-start = ((bf16[8,36,1536]{2,1,0:T(8,128)(2,1)}), bf16[8,36,1536]{2,1,0:T(8,128)(2,1)S(1)}, u32[]{:S(2)}, u32[]{:S(2)}) async-start(bf16[8,36,1536]{2,1,0:T(8,128)(2,1)} %reshape.257), calls=%async_computation | async-start | bytes 1966080 | tf_op jit(solution)/shard_map/all_to_all | solution.py:339
  174.8 49.9 %collective-permute-start.5 = (bf16[192,3072]{1,0:T(8,128)(2,1)}, bf16[192,3072]{1,0:T(8,128)(2,1)}, u32[]{:S(2)}, u32[]{:S(2)}) collective-permute-start(bf16[192,3072]{1,0:T(8,128)(2,1)} %collective-permute-done.4), channel_id=1, source_target_pairs={{0,1},{1,2},{2,3},{3,0},{4,5},{5,6},{6,7},{7,4},{8,9},{9,10},{10,1... | collective-permute-start | bytes 3538952 | tf_op jit(solution)/shard_map/ppermute | solution.py:139
  188.0 16.3 %copy-start.9 = (bf16[288,1536]{1,0:T(8,128)(2,1)}, bf16[288,1536]{1,0:T(8,128)(2,1)S(1)}, u32[]{:S(2)}) copy-start(bf16[288,1536]{1,0:T(8,128)(2,1)S(1)} %reshape.258) | copy-start | bytes 2654212
  188.1 36.6 %copy-start.65 = (bf16[1,3072,192]{1,2,0:T(8,128)(2,1)S(1)}, bf16[1,3072,192]{1,2,0:T(8,128)(2,1)}, u32[]{:S(2)}) copy-start(bf16[1,3072,192]{1,2,0:T(8,128)(2,1)} %param.26) | copy-start | bytes 3538948
  188.1 36.6 %copy-start.67 = (bf16[192,3072]{1,0:T(8,128)(2,1)S(1)}, bf16[192,3072]{1,0:T(8,128)(2,1)}, u32[]{:S(2)}) copy-start(bf16[192,3072]{1,0:T(8,128)(2,1)} %copy-done.66) | copy-start | bytes 3538948
  238.1 19.0 %all-to-all-start.1 = ((bf16[8,36,1536]{2,1,0:T(8,128)(2,1)}), bf16[8,36,1536]{2,1,0:T(8,128)(2,1)}, u32[]{:S(2)}, u32[]{:S(2)}) async-start(bf16[8,36,1536]{2,1,0:T(8,128)(2,1)} %reshape.259), calls=%async_computation.1 | async-start | bytes 1966080 | tf_op jit(solution)/shard_map/all_to_all | solution.py:353
  242.4 127.3 %all-gather.12.cloned.1.call-start = ((), (), s32[]{:S(2)}) async-start(), calls=%async_computation.7 | async-start | bytes 2064384 | tf_op jit(solution)/shard_map/all_gather | solution.py:398
  269.1 6.3 %copy-start.56 = (f32[128]{0:T(128)}, f32[128]{0:T(128)S(1)}, u32[]{:S(2)}) copy-start(f32[128]{0:T(128)S(1)} %neg.13) | copy-start | bytes 1540
  289.3 189.8 %reduce-scatter.3.cloned.1.call-start = ((), (), s32[]{:S(2)}) async-start(), calls=%async_computation.8 | async-start | bytes 5308416 | tf_op jit(solution)/shard_map/reduce_scatter | solution.py:444
  292.2 31.0 %collective-permute-start.6 = (bf16[192,3072]{1,0:T(8,128)(2,1)}, bf16[192,3072]{1,0:T(8,128)(2,1)}, u32[]{:S(2)}, u32[]{:S(2)}) collective-permute-start(bf16[192,3072]{1,0:T(8,128)(2,1)} %convolution_convert_fusion.2), channel_id=1, source_target_pairs={{0,1},{1,2},{2,3},{3,0},{4,5},{5,6},{6,7},{7,4},{8,9},{9,10},{10,1... | collective-permute-start | bytes 3538952 | tf_op jit(solution)/shard_map/ppermute | solution.py:139
  295.2 31.2 %copy-start.31 = (s32[1024]{0:T(1024)S(1)}, s32[1024]{0:T(1024)}, u32[]{:S(2)}) copy-start(s32[1024]{0:T(1024)} %copy-done.30) | copy-start | bytes 12292
  295.2 31.2 %copy-start.40 = (s32[1024]{0:T(1024)S(1)}, s32[1024]{0:T(1024)}, u32[]{:S(2)}) copy-start(s32[1024]{0:T(1024)} %param.29) | copy-start | bytes 12292
  295.2 58.9 %collective-permute-start.7 = (bf16[192,3072]{1,0:T(8,128)(2,1)}, bf16[192,3072]{1,0:T(8,128)(2,1)}, u32[]{:S(2)}, u32[]{:S(2)}) collective-permute-start(bf16[192,3072]{1,0:T(8,128)(2,1)} %convolution_convert_fusion.1), channel_id=1, source_target_pairs={{0,1},{1,2},{2,3},{3,0},{4,5},{5,6},{6,7},{7,4},{8,9},{9,10},{10,1... | collective-permute-start | bytes 3538952 | tf_op jit(solution)/shard_map/ppermute | solution.py:139
  326.4 43.2 %collective-permute-start.8 = (bf16[192,3072]{1,0:T(8,128)(2,1)}, bf16[192,3072]{1,0:T(8,128)(2,1)}, u32[]{:S(2)}, u32[]{:S(2)}) collective-permute-start(bf16[192,3072]{1,0:T(8,128)(2,1)} %add_convert_fusion.3), channel_id=1, source_target_pairs={{0,1},{1,2},{2,3},{3,0},{4,5},{5,6},{6,7},{7,4},{8,9},{9,10},{10,1... | collective-permute-start | bytes 3538952 | tf_op jit(solution)/shard_map/ppermute | solution.py:139
  339.1 13.5 %copy-start.7 = (f32[128,768]{1,0:T(8,128)S(1)}, f32[128,768]{1,0:T(8,128)}, u32[]{:S(2)}) copy-start(f32[128,768]{1,0:T(8,128)} %copy-done.6) | copy-start | bytes 1179652
  380.1 7.9 %copy-start.18 = (bf16[128,2304]{1,0:T(8,128)(2,1)S(1)}, bf16[128,2304]{1,0:T(8,128)(2,1)}, u32[]{:S(2)}) copy-start(bf16[128,2304]{1,0:T(8,128)(2,1)} %constant_dynamic-update-slice_fusion.3) | copy-start | bytes 1769476
  380.1 10.7 %copy-start.21 = (bf16[128,8,4,24]{0,3,2,1:T(8,128)(2,1)S(1)}, bf16[128,8,4,24]{0,3,2,1:T(8,128)(2,1)}, u32[]{:S(2)}) copy-start(bf16[128,8,4,24]{0,3,2,1:T(8,128)(2,1)} %copy.68) | copy-start | bytes 589828
  394.8 115.5 %reduce-scatter.5.cloned.1.call-start = ((), (), s32[]{:S(2)}) async-start(), calls=%async_computation.9 | async-start | bytes 737280 | tf_op jit(solution)/shard_map/reduce_scatter | solution.py:450
  402.9 76.3 %collective-permute-start.10 = (bf16[192,3072]{1,0:T(8,128)(2,1)}, bf16[192,3072]{1,0:T(8,128)(2,1)}, u32[]{:S(2)}, u32[]{:S(2)}) collective-permute-start(bf16[192,3072]{1,0:T(8,128)(2,1)} %add_convert_fusion.1), channel_id=1, source_target_pairs={{0,1},{1,2},{2,3},{3,0},{4,5},{5,6},{6,7},{7,4},{8,9},{9,10},{10,1... | collective-permute-start | bytes 3538952 | tf_op jit(solution)/shard_map/ppermute | solution.py:139
  406.4 7.5 %copy-start.37 = (f32[768]{0:T(1024)S(1)}, f32[768]{0:T(1024)}, u32[]{:S(2)}) copy-start(f32[768]{0:T(1024)} %param.17) | copy-start | bytes 9220
  413.8 96.5 %collective-permute-start.9 = (bf16[192,3072]{1,0:T(8,128)(2,1)}, bf16[192,3072]{1,0:T(8,128)(2,1)}, u32[]{:S(2)}, u32[]{:S(2)}) collective-permute-start(bf16[192,3072]{1,0:T(8,128)(2,1)} %add_convert_fusion.2), channel_id=1, source_target_pairs={{0,1},{1,2},{2,3},{3,0},{4,5},{5,6},{6,7},{7,4},{8,9},{9,10},{10,1... | collective-permute-start | bytes 3538952 | tf_op jit(solution)/shard_map/ppermute | solution.py:139
  479.1 55.6 %all-gather.14.cloned.1.call-start = ((), (), s32[]{:S(2)}) async-start(), calls=%async_computation.10 | async-start | bytes 1327104 | tf_op jit(solution)/shard_map/all_gather | solution.py:451
  482.5 38.6 %collective-permute-start.11 = (bf16[192,3072]{1,0:T(8,128)(2,1)}, bf16[192,3072]{1,0:T(8,128)(2,1)}, u32[]{:S(2)}, u32[]{:S(2)}) collective-permute-start(bf16[192,3072]{1,0:T(8,128)(2,1)} %add_convert_fusion), channel_id=1, source_target_pairs={{0,1},{1,2},{2,3},{3,0},{4,5},{5,6},{6,7},{7,4},{8,9},{9,10},{10,1... | collective-permute-start | bytes 3538952 | tf_op jit(solution)/shard_map/ppermute | solution.py:139
  510.3 10.8 %copy-start.5 = (f32[192,3072]{1,0:T(8,128)S(1)}, f32[192,3072]{1,0:T(8,128)}, u32[]{:S(2)}) copy-start(f32[192,3072]{1,0:T(8,128)} %fusion.51) | copy-start | bytes 7077892
  514.2 9.9 %copy-start.61 = (f32[128]{0:T(128)S(1)}, f32[128]{0:T(128)}, u32[]{:S(2)}) copy-start(f32[128]{0:T(128)} %copy-done.60) | copy-start | bytes 1540
  514.2 9.9 %copy-start.70 = (f32[128]{0:T(128)S(1)}, f32[128]{0:T(128)}, u32[]{:S(2)}) copy-start(f32[128]{0:T(128)} %get-tuple-element.87) | copy-start | bytes 1540
  514.2 9.9 %copy-start.8 = (f32[128,768]{1,0:T(8,128)S(1)}, f32[128,768]{1,0:T(8,128)}, u32[]{:S(2)}) copy-start(f32[128,768]{1,0:T(8,128)} %copy-done.6) | copy-start | bytes 1179652
  514.2 9.9 %copy-start.15 = (bf16[1,128,768]{2,1,0:T(8,128)(2,1)S(1)}, bf16[1,128,768]{2,1,0:T(8,128)(2,1)}, u32[]{:S(2)}) copy-start(bf16[1,128,768]{2,1,0:T(8,128)(2,1)} %param.15) | copy-start | bytes 589828
  514.2 9.9 %copy-start.22 = (f32[128,768]{1,0:T(8,128)S(1)}, f32[128,768]{1,0:T(8,128)}, u32[]{:S(2)}) copy-start(f32[128,768]{1,0:T(8,128)} %get-tuple-element.137) | copy-start | bytes 1179652
  514.2 9.9 %copy-start.59 = (f32[128]{0:T(128)S(1)}, f32[128]{0:T(128)}, u32[]{:S(2)}) copy-start(f32[128]{0:T(128)} %copy-done.58) | copy-start | bytes 1540
  514.2 10.8 %copy-start.24 = (f32[8064]{0:T(1024)S(1)}, f32[8064]{0:T(1024)}, u32[]{:S(2)}) copy-start(f32[8064]{0:T(1024)} %psum.7) | copy-start | bytes 96772
  (44 other events, 98.4 us)
Sparse Core Ops, SparseCore 0:
  12.0 102.8 all-gather.5
  118.6 31.1 all-gather.7
  152.3 29.7 all-gather.9
  289.4 23.1 all-gather.11
  394.9 53.7 reduce-scatter.2
  479.3 30.9 reduce-scatter.4
  512.3 22.3 all-gather.13
